TPU v7x, 32 devices: a whole 2x2x4 slice. The times are simulated.
32 devices in a mesh: space: 8 (over z, x), vel: 4 (over y, core).
Axes of the slice: x: 2, y: 2, z: 4, core: 2. Of those that a mesh axis runs over, the one named last changes fastest.
Arguments:
- dist: bfloat16 [128, 64, 4096], P('space', None, 'vel'), may hold values from -6 to 6
- send_faces: int32 [8, 2, 16], P('space'), may hold values from 0 to 95
- send_count: int32 [8, 2], P('space'), may hold values from 1 to 16, as said below
- source_face: int32 [128, 6], P('space'), may hold values from 0 to 127, as said below
- subface: int32 [128, 6], P('space'), may hold values from 0 to 4
- alpha: float32 [4, 4096], replicated, may hold values from -1 to 1
- beta: float32 [5, 4096], replicated, may hold values from -1 to 1
Outputs:
- relaxed: bfloat16 [128, 64, 4096], P('space', None, 'vel')
Inputs may be any that keep to these rules, and one draw needn't show every extreme that they name: `source_face`: for each face of a block: below 96 a local face of the same block; from 96 the 16 slots of the previous block's block toward the next one, then the 16 slots of the next block's block toward the previous one. Every slot of these two blocks is read by exactly one face of the block. `send_count`: for each direction some block's padded trace block is full. `send_faces`: local face numbers, element times 6 plus face.
All inputs are finite; a program needn't handle non-finite values.
Results may differ from a plain program's by a relative error of at most 0.0057.
Values may be sent and summed in bfloat16 or wider, within the bound.
A program may use at most 64 MiB of HBM per device.

v0:
```python
import jax
import jax.numpy as jnp
import numpy as np
from jax import lax
from jax.sharding import PartitionSpec as P

VSIDE = 16
VEL = 4096


courant = 0.1
lift_weight = 6.0
relax_step = 0.5
highest = lax.Precision.HIGHEST


def passed_along(block, axis, distance):
    devices = range(lax.axis_size(axis))
    route = [((i - distance) % len(devices), i) for i in devices]
    return lax.ppermute(block, axis, route)


def shortened(array):

    def short(part):
        return part.astype(jnp.bfloat16) if part.dtype == jnp.float32 else part

    return jax.tree.map(short, array)


def lobatto_points():
    return np.array([-1.0, -1.0 / np.sqrt(5.0), 1.0 / np.sqrt(5.0), 1.0])


def lagrange_table(targets):
    points = lobatto_points()
    result = np.ones((targets.shape[0], 4))
    for column in range(4):
        for second in range(4):
            if second != column:
                result[:, column] = (
                    result[:, column]
                    * (targets - points[second])
                    / (points[column] - points[second])
                )
    return result


def derivative_table():
    points = lobatto_points()
    result = np.zeros((4, 4))
    for row_at in range(4):
        for column in range(4):
            total = 0.0
            for skipped in range(4):
                if skipped != column:
                    factor = 1.0 / (points[column] - points[skipped])
                    for second in range(4):
                        if second != column and second != skipped:
                            factor = (
                                factor
                                * (points[row_at] - points[second])
                                / (points[column] - points[second])
                            )
                    total = total + factor
            result[row_at, column] = total
    return result


def cosine_table():
    index_list = np.arange(VSIDE)
    result = np.sqrt(2.0 / VSIDE) * np.cos(
        np.pi * (index_list[None, :] + 0.5) * index_list[:, None] / VSIDE
    )
    result[0] = result[0] / np.sqrt(2.0)
    return result


def static_tables():
    derivative = derivative_table()
    eye_four = np.eye(4)
    gradients = np.stack(
        [
            np.kron(np.kron(derivative, eye_four), eye_four),
            np.kron(np.kron(eye_four, derivative), eye_four),
            np.kron(np.kron(eye_four, eye_four), derivative),
        ]
    )
    selector = np.zeros((96, 64))
    for axis_at in range(3):
        for side_at in range(2):
            filled = 0
            for node_at in range(64):
                digits = (node_at // 16, node_at // 4 % 4, node_at % 4)
                if digits[axis_at] == 3 * side_at:
                    selector[(2 * axis_at + side_at) * 16 + filled, node_at] = 1.0
                    filled = filled + 1
    points = lobatto_points()
    halves = [lagrange_table((points - 1.0) / 2.0), lagrange_table((points + 1.0) / 2.0)]
    mortar = np.stack(
        [np.eye(16)]
        + [np.kron(halves[(which - 1) // 2], halves[(which - 1) % 2]) for which in range(1, 5)]
    )
    return (gradients, selector, mortar)


def velocity_components(first, count):
    index_list = first + jnp.arange(count)
    along = [index_list // (VSIDE * VSIDE), index_list // VSIDE % VSIDE, index_list % VSIDE]
    return jnp.stack([(entry.astype(jnp.float32) + 0.5) * (2.0 / VSIDE) - 1.0 for entry in along])


def collide_element(element, kernels, cosine, cosine_pair):
    width = element.shape[0]
    kernel_rows = kernels.shape[0]
    modes = (kernel_rows - 1) // 2
    values = element.astype(jnp.float32)
    cube = values.reshape(width, VSIDE, VSIDE * VSIDE)
    inner = jnp.einsum("nir,qr->niq", cube, cosine_pair, precision=highest)
    spectrum = jnp.einsum("ai,niq->naq", cosine, inner, precision=highest).reshape(width, 1, VEL)
    filtered = (spectrum * kernels[None]).reshape(width * kernel_rows, VSIDE, VSIDE * VSIDE)
    outer = jnp.einsum("ai,naq->niq", cosine, filtered, precision=highest)
    fields = jnp.einsum("niq,qr->nir", outer, cosine_pair, precision=highest).reshape(
        width, kernel_rows, VEL
    )
    gain = jnp.sum(fields[:, :modes] * fields[:, modes : 2 * modes], axis=1)
    loss = values * fields[:, 2 * modes]
    return (values + relax_step * (gain - loss)).astype(jnp.bfloat16)


def on_device(dist, send_faces, send_count, source_face, subface, alpha, beta):
    elements = dist.shape[0]
    vel_local = dist.shape[2]
    slots = send_faces.shape[2]
    gradients, selector, mortar = static_tables()
    grad_low = jnp.asarray(gradients, jnp.bfloat16)
    select_low = jnp.asarray(selector, jnp.bfloat16)
    select_full = jnp.asarray(selector, jnp.float32)
    mortar_low = jnp.asarray(mortar, jnp.bfloat16)
    speeds = velocity_components(lax.axis_index("vel") * vel_local, vel_local)
    rows = (
        jnp.einsum("tn,env->etv", select_low, dist, preferred_element_type=jnp.float32)
        .astype(jnp.bfloat16)
        .reshape(elements * 6, 16, vel_local)
    )
    picked = rows[send_faces[0].reshape(-1)].reshape(2, slots, 16, vel_local)
    live = jnp.arange(slots)[None, :] < send_count[0][:, None]
    outgoing = jnp.where(live[:, :, None, None], picked, jnp.zeros_like(picked))
    from_prev = passed_along(outgoing[1], "space", 1)
    from_next = passed_along(outgoing[0], "space", -1)
    drift = jnp.zeros(dist.shape, jnp.float32)
    for axis_at in range(3):
        drift = drift + speeds[axis_at] * jnp.einsum(
            "nm,emv->env", grad_low[axis_at], dist, preferred_element_type=jnp.float32
        )
    table = jnp.concatenate([rows, from_prev, from_next], axis=0)
    neighbour = table[source_face.reshape(-1)]
    projected = jnp.einsum(
        "ftu,fuv->ftv",
        mortar_low[subface.reshape(-1)],
        neighbour,
        preferred_element_type=jnp.float32,
    )
    inflow = jnp.minimum(
        jnp.stack([-speeds[0], speeds[0], -speeds[1], speeds[1], -speeds[2], speeds[2]]), 0.0
    )
    jump = (rows.astype(jnp.float32) - projected).reshape(elements, 6, 16, vel_local) * inflow[
        None, :, None, :
    ]
    lifted = jnp.einsum(
        "tn,etv->env", select_full, jump.reshape(elements, 96, vel_local), precision=highest
    )
    updated = (dist.astype(jnp.float32) - courant * drift + courant * lift_weight * lifted).astype(
        jnp.bfloat16
    )
    cosine_np = cosine_table()
    cosine = jnp.asarray(cosine_np, jnp.float32)
    cosine_pair = jnp.asarray(np.kron(cosine_np, cosine_np), jnp.float32)
    kernels = jnp.concatenate([alpha, beta], axis=0)

    def one_element(element):
        return collide_element(element, kernels, cosine, cosine_pair)

    mixed = lax.map(
        one_element, lax.all_to_all(updated, "vel", split_axis=1, concat_axis=2, tiled=True)
    )
    relaxed = lax.all_to_all(
        shortened(mixed), "vel", split_axis=2, concat_axis=1, tiled=True
    ).astype(mixed.dtype)
    return relaxed


def solution(mesh):
    return jax.shard_map(
        on_device,
        mesh=mesh,
        in_specs=(
            P("space", None, "vel"),
            P("space", None, None),
            P("space", None),
            P("space", None),
            P("space", None),
            P(),
            P(),
        ),
        out_specs=P("space", None, "vel"),
        check_vma=False,
    )
```

profile of v0, /device:TPU:27, one launch (start us, length us, event | category | flops | bytes accessed | tf_op | source)
XLA Modules:
  0.0 603.2 jit_solution(11017283849061618979)
XLA Ops:
  20.6 13.4 %collective-permute-done = bf16[16,16,1024]{2,1,0:T(8,128)(2,1)S(1)} collective-permute-done((bf16[16,16,1024]{2,1,0:T(8,128)(2,1)}, bf16[16,16,1024]{2,1,0:T(8,128)(2,1)S(1)}, u32[]{:S(2)}, u32[]{:S(2)}) %collective-permute-start) | collective-permute-done | bytes 524320 | tf_op jit(solution)/shard_map/ppermute | solution.py:20
  50.6 6.7 %fusion.5 = bf16[16,64,1024]{2,1,0:T(8,128)(2,1)S(1)} fusion(f32[64,16,1024]{2,0,1:T(8,128)S(1)} %copy-done.5, f32[64,16,1024]{2,0,1:T(8,128)S(1)} %copy-done.4, f32[64,16,1024]{2,0,1:T(8,128)S(1)} %copy-done.3, bf16[16,64,1024]{2,1,0:T(8,128)(2,1)S(1)} %copy-done, f32[16,96,1024]{2,1,0:T(8,128)S(1)} %bitcast_multiply_fusion, ...), kind=kOutput, calls=%fused_computation.17 | convolution fusion | flops 1219493888 | bytes 23105536 | tf_op jit(solution)/shard_map/tn,etv->env/dot_general | solution.py:170
  65.0 24.8 %all-to-all-done = bf16[16,64,1024]{2,0,1:T(8,128)(2,1)S(1)} async-done(((bf16[16,64,1024]{2,0,1:T(8,128)(2,1)}), bf16[16,64,1024]{2,0,1:T(8,128)(2,1)S(1)}, u32[]{:S(2)}, u32[]{:S(2)}) %all-to-all-start) | async-done | bytes 2097184 | tf_op jit(solution)/shard_map/all_to_all | solution.py:185
  91.4 415.3 %while.11 = (s32[]{:T(128)}, bf16[16,16,4096]{2,0,1:T(8,128)(2,1)}, bf16[16,16,4096]{2,0,1:T(8,128)(2,1)}, f32[9,4096]{1,0:T(8,128)S(1)}, s32[]{:T(128)}, /*inde...) while((s32[]{:T(128)}, bf16[16,16,4096]{2,0,1:T(8,128)(2,1)}, ...), condition=%wide.region_2.3_spmd.clone, body=%wide.region_0.2_spmd.sunk.clone.sunk | while | flops 2140536832 | bytes 27543648 | solution.py:184
  111.7 5.6 dynamic_update_slice.7
  137.7 5.6 dynamic_update_slice.7
  163.6 5.6 dynamic_update_slice.7
  189.6 5.6 dynamic_update_slice.7
  215.6 5.6 dynamic_update_slice.7
  241.5 5.6 dynamic_update_slice.7
  267.5 5.6 dynamic_update_slice.7
  293.4 5.6 dynamic_update_slice.7
  319.4 5.6 dynamic_update_slice.7
  345.3 5.6 dynamic_update_slice.7
  371.3 5.6 dynamic_update_slice.7
  423.2 5.6 dynamic_update_slice.7
  449.1 5.6 dynamic_update_slice.7
  475.1 5.6 dynamic_update_slice.7
  501.0 5.6 dynamic_update_slice.7
  506.7 15.3 %copy.27 = bf16[16,16,4096]{0,1,2:T(8,128)(2,1)} copy(bf16[16,16,4096]{2,0,1:T(8,128)(2,1)} %get-tuple-element.37) | data formatting | bytes 4194304 | tf_op jit(solution)/shard_map/while | solution.py:184
  522.0 19.5 %reshape.472 = bf16[4,2,131072]{2,1,0:T(2,128)(2,1)S(1)} reshape(bf16[4096,16,16]{2,1,0:T(8,128)(2,1)} %bitcast.107) | data formatting | bytes 4194304
  541.5 28.8 %all_to_all.36 = bf16[4,2,131072]{2,1,0:T(2,128)(2,1)} all-to-all(bf16[4,2,131072]{2,1,0:T(2,128)(2,1)S(1)} %reshape.472), channel_id=1, replica_groups=mesh['space'=8,'vel'=4] {'vel'}, dimensions={0} | all-to-all | bytes 4194304 | tf_op jit(solution)/shard_map/all_to_all | solution.py:187
  570.3 14.3 %reshape.473 = bf16[4096,16,16]{2,1,0:T(8,128)(2,1)} reshape(bf16[4,2,131072]{2,1,0:T(2,128)(2,1)} %all_to_all.36) | data formatting | bytes 4194304
  584.7 18.5 %copy.28 = bf16[16,4,16,1024]{3,2,1,0:T(8,128)(2,1)} copy(bf16[16,4,16,1024]{0,2,3,1:T(8,128)(2,1)} %bitcast.108) | data formatting | bytes 4194304 | tf_op jit(solution)/shard_map/all_to_all | solution.py:187
  (265 shorter events, 376.1 us)
Async XLA Ops:
  5.8 5.7 copy-start.14
  5.8 5.9 copy-start.15
  5.8 6.1 %copy-start = (bf16[16,64,1024]{2,1,0:T(8,128)(2,1)S(1)}, bf16[16,64,1024]{2,1,0:T(8,128)(2,1)}, u32[]{:S(2)}) copy-start(bf16[16,64,1024]{2,1,0:T(8,128)(2,1)} %param.15) | copy-start | bytes 6291460
  5.8 6.1 %copy-start.13 = (bf16[64,64,1]{1,0,2:T(8,128)(2,1)S(1)}, bf16[64,64,1]{1,0,2:T(8,128)(2,1)}, u32[]{:S(2)}) copy-start(bf16[64,64,1]{1,0,2:T(8,128)(2,1)} %constant.120) | copy-start | bytes 24580
  8.6 6.0 copy-start.12
  9.7 24.2 %collective-permute-start = (bf16[16,16,1024]{2,1,0:T(8,128)(2,1)}, bf16[16,16,1024]{2,1,0:T(8,128)(2,1)S(1)}, u32[]{:S(2)}, u32[]{:S(2)}) collective-permute-start(bf16[16,16,1024]{2,1,0:T(8,128)(2,1)} %get-tuple-element.63), channel_id=1, source_target_pairs={{28,0},{0,4},{4,8},{8,12},{12,16},{16,20},{20,24},{24,28},{29,1},{... | collective-permute-start | bytes 1572872 | tf_op jit(solution)/shard_map/ppermute | solution.py:20
  9.7 24.3 %collective-permute-start.1 = (bf16[16,16,1024]{2,1,0:T(8,128)(2,1)}, bf16[16,16,1024]{2,1,0:T(8,128)(2,1)}, u32[]{:S(2)}, u32[]{:S(2)}) collective-permute-start(bf16[16,16,1024]{2,1,0:T(8,128)(2,1)} %get-tuple-element.64), channel_id=1, source_target_pairs={{4,0},{8,4},{12,8},{16,12},{20,16},{24,20},{28,24},{0,28},{5,1},{9... | collective-permute-start | bytes 1572872 | tf_op jit(solution)/shard_map/ppermute | solution.py:20
  14.5 2.7 copy-start.6
  14.5 3.4 copy-start.11
  17.9 16.2 %copy-start.1 = (bf16[96,16,1024]{2,0,1:T(8,128)(2,1)S(1)}, bf16[96,16,1024]{2,0,1:T(8,128)(2,1)}, u32[]{:S(2)}) copy-start(bf16[96,16,1024]{2,0,1:T(8,128)(2,1)} %convolution_convert_fusion) | copy-start | bytes 9437188
  46.0 2.2 copy-start.3
  46.0 3.5 copy-start.4
  46.0 4.6 copy-start.5
  46.0 4.6 copy-start.10
  57.3 7.7 %copy-start.8 = (f32[5,4096]{1,0:T(8,128)S(1)}, f32[5,4096]{1,0:T(8,128)}, u32[]{:S(2)}) copy-start(f32[5,4096]{1,0:T(8,128)} %param.21) | copy-start | bytes 245764
  57.3 7.7 %copy-start.9 = (f32[4,4096]{1,0:T(4,128)S(1)}, f32[4,4096]{1,0:T(4,128)}, u32[]{:S(2)}) copy-start(f32[4,4096]{1,0:T(4,128)} %param.20) | copy-start | bytes 196612
  59.8 31.6 %copy-start.2 = (f32[256,256,1]{1,0,2:T(8,128)S(1)}, f32[256,256,1]{1,0,2:T(8,128)}, u32[]{:S(2)}) copy-start(f32[256,256,1]{1,0,2:T(8,128)} %constant.234) | copy-start | bytes 786436
  59.8 31.6 %copy-start.7 = (f32[16,16,1]{1,0,2:T(8,128)S(1)}, f32[16,16,1]{1,0,2:T(8,128)}, u32[]{:S(2)}) copy-start(f32[16,16,1]{1,0,2:T(8,128)} %constant.235) | copy-start | bytes 3076
  59.8 30.0 %all-to-all-start = ((bf16[16,64,1024]{2,0,1:T(8,128)(2,1)}), bf16[16,64,1024]{2,0,1:T(8,128)(2,1)S(1)}, u32[]{:S(2)}, u32[]{:S(2)}) async-start(bf16[16,64,1024]{2,0,1:T(8,128)(2,1)} %copy.25), calls=%async_computation | async-start | bytes 4194304 | tf_op jit(solution)/shard_map/all_to_all | solution.py:185
where the time goes:
time: 611 us; the launch traced here: 603 us
  local copies, waits for them, and re-layouts  294 us (48%)
  other arithmetic  134 us (22%)
  matrix products  101 us (17%)
  waiting for transfers between devices  38.3 us (6%)
  blocking collectives  28.8 us (5%)
  starting transfers between devices  6.62 us (1%)
    dynamic_update_slice x16, local copies, waits for them, and re-layouts, on_device(): lax.map(one_element, lax.all_to_all(updated, 'vel', split_axis=1, concat_...  90 us
    reduce_sum x16, other arithmetic, collide_element(): gain = jnp.sum(fields[:, :modes] * fields[:, modes:2 * modes], axis=1)  50.3 us
    mul x16, local copies, waits for them, and re-layouts, collide_element(): spectrum * kernels[None]  47.9 us
    convert_element_type x16, other arithmetic, collide_element(): return (values + relax_step * (gain - loss)).astype(jnp.bfloat16)  38.9 us
    mul x16, other arithmetic, collide_element(): spectrum * kernels[None]  38.8 us
    unnamed x36, local copies, waits for them, and re-layouts  37.3 us
    reshape x16, local copies, waits for them, and re-layouts, collide_element(): jnp.einsum('niq,qr->nir', outer, cosine_pair, precision=highest)  35.1 us
    dot_general x16, matrix products, collide_element(): outer = jnp.einsum('ai,naq->niq', cosine, filtered, precision=highest)  34.8 us
  transfers between devices with their start and end apart: 3, of which 3 were waited for; matrix products, arithmetic and copies ran while one was open for 2% of the time, Pallas kernels for 0%

commit v1 on v0

v1 whole, which is shorter than its diff:
```python
import jax
import jax.numpy as jnp
import numpy as np
from jax import lax
from jax.experimental import pallas as pl
from jax.experimental.pallas import tpu as pltpu
from jax.sharding import PartitionSpec as P

VSIDE = 16
VEL = 4096


courant = 0.1
lift_weight = 6.0
relax_step = 0.5


def passed_along(block, axis, distance):
    devices = range(lax.axis_size(axis))
    route = [((i - distance) % len(devices), i) for i in devices]
    return lax.ppermute(block, axis, route)


def lobatto_points():
    return np.array([-1.0, -1.0 / np.sqrt(5.0), 1.0 / np.sqrt(5.0), 1.0])


def lagrange_table(targets):
    points = lobatto_points()
    result = np.ones((targets.shape[0], 4))
    for column in range(4):
        for second in range(4):
            if second != column:
                result[:, column] = (
                    result[:, column]
                    * (targets - points[second])
                    / (points[column] - points[second])
                )
    return result


def derivative_table():
    points = lobatto_points()
    result = np.zeros((4, 4))
    for row_at in range(4):
        for column in range(4):
            total = 0.0
            for skipped in range(4):
                if skipped != column:
                    factor = 1.0 / (points[column] - points[skipped])
                    for second in range(4):
                        if second != column and second != skipped:
                            factor = (
                                factor
                                * (points[row_at] - points[second])
                                / (points[column] - points[second])
                            )
                    total = total + factor
            result[row_at, column] = total
    return result


def cosine_table():
    index_list = np.arange(VSIDE)
    result = np.sqrt(2.0 / VSIDE) * np.cos(
        np.pi * (index_list[None, :] + 0.5) * index_list[:, None] / VSIDE
    )
    result[0] = result[0] / np.sqrt(2.0)
    return result


def static_tables():
    derivative = derivative_table()
    eye_four = np.eye(4)
    gradients = np.stack(
        [
            np.kron(np.kron(derivative, eye_four), eye_four),
            np.kron(np.kron(eye_four, derivative), eye_four),
            np.kron(np.kron(eye_four, eye_four), derivative),
        ]
    )
    selector = np.zeros((96, 64))
    for axis_at in range(3):
        for side_at in range(2):
            filled = 0
            for node_at in range(64):
                digits = (node_at // 16, node_at // 4 % 4, node_at % 4)
                if digits[axis_at] == 3 * side_at:
                    selector[(2 * axis_at + side_at) * 16 + filled, node_at] = 1.0
                    filled = filled + 1
    points = lobatto_points()
    halves = [lagrange_table((points - 1.0) / 2.0), lagrange_table((points + 1.0) / 2.0)]
    mortar = np.stack(
        [np.eye(16)]
        + [np.kron(halves[(which - 1) // 2], halves[(which - 1) % 2]) for which in range(1, 5)]
    )
    return (gradients, selector, mortar)


def velocity_components(first, count):
    index_list = first + jnp.arange(count)
    along = [index_list // (VSIDE * VSIDE), index_list // VSIDE % VSIDE, index_list % VSIDE]
    return jnp.stack([(entry.astype(jnp.float32) + 0.5) * (2.0 / VSIDE) - 1.0 for entry in along])


def face_parts():
    gradients, selector, mortar = static_tables()
    low = jnp.bfloat16
    grad = np.asarray(gradients.reshape(192, 64).astype(low), np.float64)
    mort = np.asarray(mortar.astype(low), np.float64)
    levels = mort.shape[0]
    spread = np.zeros((levels, 192, 96))
    for face in range(6):
        sel = selector[16 * face : 16 * face + 16]
        for level in range(levels):
            spread[level, 64 * (face // 2) : 64 * (face // 2) + 64, 16 * face : 16 * face + 16] = (
                sel.T @ mort[level]
            )
    stacked = np.concatenate(
        [np.broadcast_to(grad, (levels, 192, 64)), 4.0 * spread, 2.0 * spread], axis=2
    )
    return stacked, selector


def trace_kernel(send_ref, count_ref, select_ref, dist_ref, table_ref, out_ref):
    elements = dist_ref.shape[0]
    slots = out_ref.shape[1]

    def fill(e, carry):
        got = jnp.dot(select_ref[...], dist_ref[e], preferred_element_type=jnp.float32)
        table_ref[pl.ds(6 * e, 6)] = got.astype(jnp.bfloat16).reshape(6, 16, got.shape[1])
        return carry

    lax.fori_loop(0, elements, fill, 0)

    def pick(k, carry):
        j = k // slots
        m = k % slots
        got = table_ref[send_ref[j, m]]
        live = (m < count_ref[j]).astype(jnp.bfloat16)
        out_ref[j, m] = got * live
        return carry

    lax.fori_loop(0, 2 * slots, pick, 0)


def transport_kernel(
    source_ref, dist_ref, table_ref, prev_ref, next_ref, w_ref, coef_ref, scale_ref, mask_ref,
    out_ref, full, block,
):
    elements = dist_ref.shape[0]
    local = table_ref.shape[0]
    slots = prev_ref.shape[0]
    full[0:local] = table_ref[...]
    full[local : local + slots] = prev_ref[...]
    full[local + slots : local + 2 * slots] = next_ref[...]

    def step(e, carry):
        here = dist_ref[e]
        block[0:64] = here
        for face in range(6):
            got = full[source_ref[e, face]] * mask_ref[face : face + 1, :]
            block[64 + 16 * face : 80 + 16 * face] = got
            block[160 + 16 * face : 176 + 16 * face] = got
        moved = jnp.dot(w_ref[e], block[...], preferred_element_type=jnp.float32)
        total = coef_ref[...] * here.astype(jnp.float32)
        for axis_at in range(3):
            total = total + scale_ref[axis_at : axis_at + 1, :] * moved[64 * axis_at : 64 * axis_at + 64]
        out_ref[e] = total.astype(jnp.bfloat16)
        return carry

    lax.fori_loop(0, elements, step, 0)


def collide_block(values, kernels, pair_t, pair, outer, outer_t):
    low = jnp.bfloat16
    inner = jnp.dot(values, pair_t, preferred_element_type=jnp.float32).astype(low)
    spectrum = jnp.dot(outer, inner, preferred_element_type=jnp.float32).reshape(16, 16, 256)
    rows = kernels.shape[0]
    modes = (rows - 1) // 2

    def field(m):
        scaled = (spectrum * kernels[m][:, None, :]).astype(low).reshape(256, 256)
        back = jnp.dot(scaled, pair, preferred_element_type=jnp.float32).astype(low)
        return jnp.dot(outer_t, back, preferred_element_type=jnp.float32)

    wide = values.astype(jnp.float32)
    total = -wide * field(2 * modes)
    for m in range(modes):
        total = total + field(m) * field(modes + m)
    return (wide + relax_step * total).astype(low)


def collide_kernel(x_ref, kernel_ref, pair_t_ref, pair_ref, outer_ref, outer_t_ref, out_ref):
    sources = x_ref.shape[0]
    per = x_ref.shape[3] // 256
    parts = [
        x_ref[s, 0, :, 256 * q : 256 * q + 256] for s in range(sources) for q in range(per)
    ]
    values = jnp.concatenate(parts, axis=0)
    got = collide_block(
        values, kernel_ref, pair_t_ref[...], pair_ref[...], outer_ref[...], outer_t_ref[...]
    )
    for s in range(sources):
        for q in range(per):
            at = 16 * (per * s + q)
            out_ref[s, 0, :, 256 * q : 256 * q + 256] = got[at : at + 16]


def on_device(dist, send_faces, send_count, source_face, subface, alpha, beta):
    low = jnp.bfloat16
    elements = dist.shape[0]
    vel_local = dist.shape[2]
    slots = send_faces.shape[2]
    ranks = lax.axis_size("vel")
    smem = pl.BlockSpec(memory_space=pltpu.SMEM)
    vmem = pl.BlockSpec(memory_space=pltpu.VMEM)
    stacked, selector = face_parts()
    params = pltpu.CompilerParams(vmem_limit_bytes=48 * 1024 * 1024)

    table, outgoing = pl.pallas_call(
        trace_kernel,
        out_shape=(
            jax.ShapeDtypeStruct((elements * 6, 16, vel_local), low),
            jax.ShapeDtypeStruct((2, slots, 16, vel_local), low),
        ),
        in_specs=[smem, smem, vmem, vmem],
        out_specs=(vmem, vmem),
        compiler_params=params,
    )(send_faces[0], send_count[0], jnp.asarray(selector, low), dist)
    from_prev = passed_along(outgoing[1], "space", 1)
    from_next = passed_along(outgoing[0], "space", -1)

    speeds = velocity_components(lax.axis_index("vel") * vel_local, vel_local)
    column_level = jnp.concatenate(
        [jnp.zeros((elements, 64), subface.dtype)] + [jnp.repeat(subface, 16, axis=1)] * 2, axis=1
    )
    weights = jnp.zeros((elements, 192, 256), low)
    for level in range(stacked.shape[0]):
        weights = jnp.where(
            column_level[:, None, :] == level, jnp.asarray(stacked[level], low)[None], weights
        )
    digits = np.stack([np.arange(64) // 16, np.arange(64) // 4 % 4, np.arange(64) % 4])
    first = jnp.asarray(digits == 0, jnp.float32)[:, :, None]
    last = jnp.asarray(digits == 3, jnp.float32)[:, :, None]
    up = jnp.maximum(speeds, 0.0)[:, None, :]
    down = jnp.minimum(speeds, 0.0)[:, None, :]
    coef = 1.0 + courant * lift_weight * jnp.sum(last * down - first * up, axis=0)
    mask = jnp.stack(
        [-(speeds > 0).astype(low), (speeds < 0).astype(low)], axis=1
    ).reshape(6, vel_local)
    scale = -courant * speeds

    updated = pl.pallas_call(
        transport_kernel,
        out_shape=jax.ShapeDtypeStruct(dist.shape, low),
        in_specs=[smem] + [vmem] * 8,
        out_specs=vmem,
        scratch_shapes=[
            pltpu.VMEM((elements * 6 + 2 * slots, 16, vel_local), low),
            pltpu.VMEM((256, vel_local), low),
        ],
        compiler_params=params,
    )(source_face, dist, table, from_prev, from_next, weights, coef, scale, mask)

    cosine = cosine_table()
    pair = np.kron(cosine, cosine)
    outer = np.kron(cosine, np.eye(16))
    tables = [jnp.asarray(t, low) for t in (pair.T, pair, outer, outer.T)]
    kernels = jnp.concatenate([alpha, beta], axis=0)
    kernels = kernels.reshape(kernels.shape[0], VSIDE, VSIDE * VSIDE)

    share = elements // ranks
    gathered = lax.all_to_all(
        updated.reshape(ranks, share, 64, vel_local), "vel", split_axis=0, concat_axis=0
    )
    blockspec = pl.BlockSpec((ranks, 1, 16, vel_local), lambda e, g: (0, e, g, 0))
    mixed = pl.pallas_call(
        collide_kernel,
        grid=(share, 4),
        out_shape=jax.ShapeDtypeStruct(gathered.shape, low),
        in_specs=[blockspec] + [vmem] * 5,
        out_specs=blockspec,
        compiler_params=params,
    )(gathered, kernels, *tables)
    relaxed = lax.all_to_all(mixed, "vel", split_axis=0, concat_axis=0)
    return relaxed.reshape(dist.shape)


def solution(mesh):
    return jax.shard_map(
        on_device,
        mesh=mesh,
        in_specs=(
            P("space", None, "vel"),
            P("space", None, None),
            P("space", None),
            P("space", None),
            P("space", None),
            P(),
            P(),
        ),
        out_specs=P("space", None, "vel"),
        check_vma=False,
    )
```

time: 611 us -> 127 us (0.21)
  the two profiles are of different devices: /device:TPU:27 before, /device:TPU:0 now
where the time goes in v1:
time: 127 us; the launch traced here: 126 us
  waiting for transfers between devices  45.4 us (36%)
  Pallas kernels  34.5 us (27%)
  blocking collectives  28.2 us (22%)
  starting transfers between devices  9.86 us (8%)
  local copies, waits for them, and re-layouts  6.88 us (5%)
    all_to_all x1, blocking collectives, on_device(): relaxed = lax.all_to_all(mixed, 'vel', split_axis=0, concat_axis=0)  28.2 us
    all_to_all x1, waiting for transfers between devices, on_device(): lax.all_to_all(updated.reshape(ranks, share, 64, vel_local), 'vel', split...  25.5 us
    pallas_call x1, Pallas kernels, on_device(): pl.pallas_call(collide_kernel, grid=(share, 4), out_shape=jax.ShapeDtypeS...  21.4 us
    ppermute x2, waiting for transfers between devices, passed_along(): return lax.ppermute(block, axis, route)  19.9 us
    pallas_call x1, Pallas kernels, on_device(): pl.pallas_call(transport_kernel, out_shape=jax.ShapeDtypeStruct(dist.shap...  7.22 us
    unnamed x44, local copies, waits for them, and re-layouts  6.62 us
    ppermute x2, starting transfers between devices, passed_along(): return lax.ppermute(block, axis, route)  6.11 us
    pallas_call x1, Pallas kernels, on_device(): pl.pallas_call(trace_kernel, out_shape=(jax.ShapeDtypeStruct((elements *...  5.87 us
  transfers between devices with their start and end apart: 3, of which 3 were waited for; matrix products, arithmetic and copies ran while one was open for 1% of the time, Pallas kernels for 0%

profile of v1, /device:TPU:0, one launch (start us, length us, event | category | flops | bytes accessed | tf_op | source)
XLA Modules:
  0.0 126.2 jit_solution(3133650657309457954)
XLA Ops:
  0.0 1.6 %copy-done = bf16[16,64,1024]{2,1,0:T(8,128)(2,1)S(1)} copy-done((bf16[16,64,1024]{2,1,0:T(8,128)(2,1)S(1)}, bf16[16,64,1024]{2,1,0:T(8,128)(2,1)}, u32[]{:S(2)}) %copy-start) | copy-done | bytes 2097176
  1.6 0.7 copy-done.6
  2.3 0.7 copy-done.7
  3.0 0.7 copy-done.8
  3.7 5.9 %shard_map.181 = (bf16[96,16,1024]{2,1,0:T(8,128)(2,1)}, bf16[2,16,16,1024]{3,2,1,0:T(8,128)(2,1)S(1)}) custom-call(s32[2,16]{1,0:T(2,128)S(1)} %bitcast.18, s32[2]{0:T(128)S(1)} %bitcast.19, bf16[96,64]{1,0:T(8,128)(2,1)S(1)} %copy-done.6, bf16[16,64,1024]{2,1,0:T(8,128)(2,1)S(1)} %copy-done), custom_call_target="tpu_custom_call" | custom-call | tf_op jit(solution)/shard_map/pallas_call | solution.py:221
  9.7 3.0 %collective-permute-start = (bf16[16,16,1024]{2,1,0:T(8,128)(2,1)S(1)}, bf16[16,16,1024]{2,1,0:T(8,128)(2,1)S(1)}, u32[]{:S(2)}, u32[]{:S(2)}) collective-permute-start(bf16[16,16,1024]{2,1,0:T(8,128)(2,1)S(1)} %get-tuple-element.12), channel_id=1, source_target_pairs={{28,0},{0,4},{4,8},{8,12},{12,16},{16,20},{20,24},{24,28},{29,1},{... | collective-permute-start | bytes 1572872 | tf_op jit(solution)/shard_map/ppermute | solution.py:21
  12.7 3.1 %collective-permute-start.1 = (bf16[16,16,1024]{2,1,0:T(8,128)(2,1)S(1)}, bf16[16,16,1024]{2,1,0:T(8,128)(2,1)S(1)}, u32[]{:S(2)}, u32[]{:S(2)}) collective-permute-start(bf16[16,16,1024]{2,1,0:T(8,128)(2,1)S(1)} %get-tuple-element.11), channel_id=1, source_target_pairs={{4,0},{8,4},{12,8},{16,12},{20,16},{24,20},{28,24},{0,28},{5,1},{9... | collective-permute-start | bytes 1572872 | tf_op jit(solution)/shard_map/ppermute | solution.py:21
  16.1 0.2 subtract_reduce_fusion
  16.4 0.1 copy.24
  16.5 0.1 broadcast_in_dim.80
  16.6 0.1 concatenate.50
  16.7 0.1 copy.25.source_ref
  16.8 0.1 fusion.4
  16.9 0.5 select_select_fusion.w_ref
  17.4 17.7 %collective-permute-done.prev_ref = bf16[16,16,1024]{2,1,0:T(8,128)(2,1)S(1)} collective-permute-done((bf16[16,16,1024]{2,1,0:T(8,128)(2,1)S(1)}, bf16[16,16,1024]{2,1,0:T(8,128)(2,1)S(1)}, u32[]{:S(2)}, u32[]{:S(2)}) %collective-permute-start) | collective-permute-done | bytes 524320 | tf_op jit(solution)/shard_map/ppermute | solution.py:21
  35.1 2.2 %collective-permute-done.1.next_ref = bf16[16,16,1024]{2,1,0:T(8,128)(2,1)S(1)} collective-permute-done((bf16[16,16,1024]{2,1,0:T(8,128)(2,1)S(1)}, bf16[16,16,1024]{2,1,0:T(8,128)(2,1)S(1)}, u32[]{:S(2)}, u32[]{:S(2)}) %collective-permute-start.1) | collective-permute-done | bytes 524320 | tf_op jit(solution)/shard_map/ppermute | solution.py:21
  37.3 7.2 %shard_map.182 = bf16[16,64,1024]{2,1,0:T(8,128)(2,1)S(1)} custom-call(s32[16,6]{1,0:T(8,128)S(1)} %copy.25.source_ref, bf16[16,64,1024]{2,1,0:T(8,128)(2,1)} %dist_ref.3, bf16[96,16,1024]{2,1,0:T(8,128)(2,1)} %get-tuple-element.7.table_ref, bf16[16,16,1024]{2,1,0:T(8,128)(2,1)S(1)} %collective-permute-done.prev_ref, ...), custom_call_target="tpu_custom_call" | custom-call | tf_op jit(solution)/shard_map/pallas_call | solution.py:254
  44.6 1.3 %copy-done.1 = bf16[16,64,1024]{2,1,0:T(8,128)(2,1)} copy-done((bf16[16,64,1024]{2,1,0:T(8,128)(2,1)}, bf16[16,64,1024]{2,1,0:T(8,128)(2,1)S(1)}, u32[]{:S(2)}) %copy-start.1) | copy-done | bytes 2097176
  45.9 3.8 %all-to-all-start = ((bf16[4,4,64,1024]{3,2,1,0:T(8,128)(2,1)}), bf16[4,4,64,1024]{3,2,1,0:T(8,128)(2,1)S(1)}, u32[]{:S(2)}, u32[]{:S(2)}) async-start(bf16[4,4,64,1024]{3,2,1,0:T(8,128)(2,1)} %bitcast.17), calls=%async_computation | async-start | bytes 4194304 | tf_op jit(solution)/shard_map/all_to_all | solution.py:274
  49.7 0.1 copy.26
  49.8 25.5 %all-to-all-done.x_ref = bf16[4,4,64,1024]{3,2,1,0:T(8,128)(2,1)S(1)} async-done(((bf16[4,4,64,1024]{3,2,1,0:T(8,128)(2,1)}), bf16[4,4,64,1024]{3,2,1,0:T(8,128)(2,1)S(1)}, u32[]{:S(2)}, u32[]{:S(2)}) %all-to-all-start) | async-done | bytes 2097184 | tf_op jit(solution)/shard_map/all_to_all | solution.py:274
  75.3 21.4 %shard_map.183 = bf16[4,4,64,1024]{3,2,1,0:T(8,128)(2,1)S(1)} custom-call(bf16[4,4,64,1024]{3,2,1,0:T(8,128)(2,1)S(1)} %all-to-all-done.x_ref, f32[9,16,256]{2,1,0:T(8,128)S(1)} %slice.8.kernel_ref, bf16[256,256]{1,0:T(8,128)(2,1)S(1)} %copy-done.2, bf16[256,256]{1,0:T(8,128)(2,1)S(1)} %copy-done.3, bf16[256,256]{1,0:T(8,128)(2,1)S(1)} %copy-done.4, ...), custom_call_target="tpu_custom_call" | custom-call | tf_op jit(solution)/shard_map/pallas_call | solution.py:278
  96.8 28.2 %all_to_all.10 = bf16[4,4,64,1024]{3,2,1,0:T(8,128)(2,1)S(1)} all-to-all(bf16[4,4,64,1024]{3,2,1,0:T(8,128)(2,1)S(1)} %shard_map.183), channel_id=1, replica_groups=mesh['space'=8,'vel'=4] {'vel'}, dimensions={0} | all-to-all | bytes 4194304 | tf_op jit(solution)/shard_map/all_to_all | solution.py:286
  124.9 1.3 %copy.28 = bf16[16,64,1024]{2,1,0:T(8,128)(2,1)} copy(bf16[16,64,1024]{2,1,0:T(8,128)(2,1)S(1)} %bitcast.20) | data formatting | bytes 4194304
  (50 shorter events, 0.6 us)
Async XLA Ops:
  0.0 1.6 %copy-start = (bf16[16,64,1024]{2,1,0:T(8,128)(2,1)S(1)}, bf16[16,64,1024]{2,1,0:T(8,128)(2,1)}, u32[]{:S(2)}) copy-start(bf16[16,64,1024]{2,1,0:T(8,128)(2,1)} %dist_ref.3) | copy-start | bytes 6291460
  1.6 0.7 copy-start.6
  2.3 0.7 copy-start.7
  3.0 0.7 copy-start.8
  9.5 6.5 %copy-start.18 = (f32[3,64]{1,0:T(4,128)S(1)}, f32[3,64]{1,0:T(4,128)}, u32[]{:S(2)}) copy-start(f32[3,64]{1,0:T(4,128)} %constant.108.clone) | copy-start | bytes 2308
  9.5 6.5 %copy-start.19 = (f32[3,64]{1,0:T(4,128)S(1)}, f32[3,64]{1,0:T(4,128)}, u32[]{:S(2)}) copy-start(f32[3,64]{1,0:T(4,128)} %constant.109.clone) | copy-start | bytes 2308
  9.5 6.9 %copy-start.16 = (s32[16,6]{0,1:T(8,128)S(1)}, s32[16,6]{0,1:T(8,128)}, u32[]{:S(2)}) copy-start(s32[16,6]{0,1:T(8,128)} %param.23) | copy-start | bytes 1156
  9.5 7.1 %copy-start.17 = (s32[16,6]{0,1:T(8,128)S(1)}, s32[16,6]{0,1:T(8,128)}, u32[]{:S(2)}) copy-start(s32[16,6]{0,1:T(8,128)} %param.22) | copy-start | bytes 1156
  9.6 7.3 %copy-start.10 = (bf16[192,256]{1,0:T(8,128)(2,1)S(1)}, bf16[192,256]{1,0:T(8,128)(2,1)}, u32[]{:S(2)}) copy-start(bf16[192,256]{1,0:T(8,128)(2,1)} %constant.103.clone) | copy-start | bytes 294916
  9.6 7.3 %copy-start.11 = (bf16[192,256]{1,0:T(8,128)(2,1)S(1)}, bf16[192,256]{1,0:T(8,128)(2,1)}, u32[]{:S(2)}) copy-start(bf16[192,256]{1,0:T(8,128)(2,1)} %constant.104.clone) | copy-start | bytes 294916
  9.6 7.3 %copy-start.12 = (bf16[192,256]{1,0:T(8,128)(2,1)S(1)}, bf16[192,256]{1,0:T(8,128)(2,1)}, u32[]{:S(2)}) copy-start(bf16[192,256]{1,0:T(8,128)(2,1)} %constant.105.clone) | copy-start | bytes 294916
  9.6 7.3 %copy-start.13 = (bf16[192,256]{1,0:T(8,128)(2,1)S(1)}, bf16[192,256]{1,0:T(8,128)(2,1)}, u32[]{:S(2)}) copy-start(bf16[192,256]{1,0:T(8,128)(2,1)} %constant.106.clone) | copy-start | bytes 294916
  9.6 7.3 %copy-start.14 = (bf16[192,256]{1,0:T(8,128)(2,1)S(1)}, bf16[192,256]{1,0:T(8,128)(2,1)}, u32[]{:S(2)}) copy-start(bf16[192,256]{1,0:T(8,128)(2,1)} %constant.107.clone) | copy-start | bytes 294916
  9.7 25.4 %collective-permute-start = (bf16[16,16,1024]{2,1,0:T(8,128)(2,1)S(1)}, bf16[16,16,1024]{2,1,0:T(8,128)(2,1)S(1)}, u32[]{:S(2)}, u32[]{:S(2)}) collective-permute-start(bf16[16,16,1024]{2,1,0:T(8,128)(2,1)S(1)} %get-tuple-element.12), channel_id=1, source_target_pairs={{28,0},{0,4},{4,8},{8,12},{12,16},{16,20},{20,24},{24,28},{29,1},{... | collective-permute-start | bytes 1572872 | tf_op jit(solution)/shard_map/ppermute | solution.py:21
  12.7 24.6 %collective-permute-start.1 = (bf16[16,16,1024]{2,1,0:T(8,128)(2,1)S(1)}, bf16[16,16,1024]{2,1,0:T(8,128)(2,1)S(1)}, u32[]{:S(2)}, u32[]{:S(2)}) collective-permute-start(bf16[16,16,1024]{2,1,0:T(8,128)(2,1)S(1)} %get-tuple-element.11), channel_id=1, source_target_pairs={{4,0},{8,4},{12,8},{16,12},{20,16},{24,20},{28,24},{0,28},{5,1},{9... | collective-permute-start | bytes 1572872 | tf_op jit(solution)/shard_map/ppermute | solution.py:21
  44.5 1.3 %copy-start.1 = (bf16[16,64,1024]{2,1,0:T(8,128)(2,1)}, bf16[16,64,1024]{2,1,0:T(8,128)(2,1)S(1)}, u32[]{:S(2)}) copy-start(bf16[16,64,1024]{2,1,0:T(8,128)(2,1)S(1)} %shard_map.182) | copy-start | bytes 6291460
  45.9 3.8 %copy-start.9 = (f32[5,4096]{1,0:T(8,128)S(1)}, f32[5,4096]{1,0:T(8,128)}, u32[]{:S(2)}) copy-start(f32[5,4096]{1,0:T(8,128)} %param.25) | copy-start | bytes 245764
  45.9 3.8 %copy-start.15 = (f32[4,4096]{1,0:T(4,128)S(1)}, f32[4,4096]{1,0:T(4,128)}, u32[]{:S(2)}) copy-start(f32[4,4096]{1,0:T(4,128)} %param.24) | copy-start | bytes 196612
  45.9 29.5 %copy-start.2 = (bf16[256,256]{1,0:T(8,128)(2,1)S(1)}, bf16[256,256]{1,0:T(8,128)(2,1)}, u32[]{:S(2)}) copy-start(bf16[256,256]{1,0:T(8,128)(2,1)} %constant.110.clone.pair_t_ref) | copy-start | bytes 393220
  45.9 29.5 %copy-start.3 = (bf16[256,256]{1,0:T(8,128)(2,1)S(1)}, bf16[256,256]{1,0:T(8,128)(2,1)}, u32[]{:S(2)}) copy-start(bf16[256,256]{1,0:T(8,128)(2,1)} %constant.111.clone.pair_ref) | copy-start | bytes 393220
  45.9 29.5 %copy-start.4 = (bf16[256,256]{1,0:T(8,128)(2,1)S(1)}, bf16[256,256]{1,0:T(8,128)(2,1)}, u32[]{:S(2)}) copy-start(bf16[256,256]{1,0:T(8,128)(2,1)} %constant.112.clone.outer_ref) | copy-start | bytes 393220
  45.9 29.5 %copy-start.5 = (bf16[256,256]{1,0:T(8,128)(2,1)S(1)}, bf16[256,256]{1,0:T(8,128)(2,1)}, u32[]{:S(2)}) copy-start(bf16[256,256]{1,0:T(8,128)(2,1)} %constant.113.clone.outer_t_ref) | copy-start | bytes 393220
  45.9 29.4 %all-to-all-start = ((bf16[4,4,64,1024]{3,2,1,0:T(8,128)(2,1)}), bf16[4,4,64,1024]{3,2,1,0:T(8,128)(2,1)S(1)}, u32[]{:S(2)}, u32[]{:S(2)}) async-start(bf16[4,4,64,1024]{3,2,1,0:T(8,128)(2,1)} %bitcast.17), calls=%async_computation | async-start | bytes 4194304 | tf_op jit(solution)/shard_map/all_to_all | solution.py:274

commit v2 on v1

--- a/solution.py
+++ b/solution.py
@@ -1,3 +1,5 @@
+import functools
+
 import jax
 import jax.numpy as jnp
 import numpy as np
@@ -13,12 +15,7 @@
 courant = 0.1
 lift_weight = 6.0
 relax_step = 0.5
-
-
-def passed_along(block, axis, distance):
-    devices = range(lax.axis_size(axis))
-    route = [((i - distance) % len(devices), i) for i in devices]
-    return lax.ppermute(block, axis, route)
+MESH = pl.DeviceIdType.MESH
 
 
 def lobatto_points():
@@ -122,56 +119,6 @@
     return stacked, selector
 
 
-def trace_kernel(send_ref, count_ref, select_ref, dist_ref, table_ref, out_ref):
-    elements = dist_ref.shape[0]
-    slots = out_ref.shape[1]
-
-    def fill(e, carry):
-        got = jnp.dot(select_ref[...], dist_ref[e], preferred_element_type=jnp.float32)
-        table_ref[pl.ds(6 * e, 6)] = got.astype(jnp.bfloat16).reshape(6, 16, got.shape[1])
-        return carry
-
-    lax.fori_loop(0, elements, fill, 0)
-
-    def pick(k, carry):
-        j = k // slots
-        m = k % slots
-        got = table_ref[send_ref[j, m]]
-        live = (m < count_ref[j]).astype(jnp.bfloat16)
-        out_ref[j, m] = got * live
-        return carry
-
-    lax.fori_loop(0, 2 * slots, pick, 0)
-
-
-def transport_kernel(
-    source_ref, dist_ref, table_ref, prev_ref, next_ref, w_ref, coef_ref, scale_ref, mask_ref,
-    out_ref, full, block,
-):
-    elements = dist_ref.shape[0]
-    local = table_ref.shape[0]
-    slots = prev_ref.shape[0]
-    full[0:local] = table_ref[...]
-    full[local : local + slots] = prev_ref[...]
-    full[local + slots : local + 2 * slots] = next_ref[...]
-
-    def step(e, carry):
-        here = dist_ref[e]
-        block[0:64] = here
-        for face in range(6):
-            got = full[source_ref[e, face]] * mask_ref[face : face + 1, :]
-            block[64 + 16 * face : 80 + 16 * face] = got
-            block[160 + 16 * face : 176 + 16 * face] = got
-        moved = jnp.dot(w_ref[e], block[...], preferred_element_type=jnp.float32)
-        total = coef_ref[...] * here.astype(jnp.float32)
-        for axis_at in range(3):
-            total = total + scale_ref[axis_at : axis_at + 1, :] * moved[64 * axis_at : 64 * axis_at + 64]
-        out_ref[e] = total.astype(jnp.bfloat16)
-        return carry
-
-    lax.fori_loop(0, elements, step, 0)
-
-
 def collide_block(values, kernels, pair_t, pair, outer, outer_t):
     low = jnp.bfloat16
     inner = jnp.dot(values, pair_t, preferred_element_type=jnp.float32).astype(low)
@@ -191,20 +138,134 @@
     return (wide + relax_step * total).astype(low)
 
 
-def collide_kernel(x_ref, kernel_ref, pair_t_ref, pair_ref, outer_ref, outer_t_ref, out_ref):
-    sources = x_ref.shape[0]
-    per = x_ref.shape[3] // 256
-    parts = [
-        x_ref[s, 0, :, 256 * q : 256 * q + 256] for s in range(sources) for q in range(per)
-    ]
-    values = jnp.concatenate(parts, axis=0)
-    got = collide_block(
-        values, kernel_ref, pair_t_ref[...], pair_ref[...], outer_ref[...], outer_t_ref[...]
-    )
-    for s in range(sources):
-        for q in range(per):
-            at = 16 * (per * s + q)
-            out_ref[s, 0, :, 256 * q : 256 * q + 256] = got[at : at + 16]
+def fused_kernel(
+    sizes, send_ref, count_ref, source_ref, dist_ref, select_ref, w_ref, coef_ref, scale_ref,
+    mask_ref, kernel_ref, pair_t_ref, pair_ref, outer_ref, outer_t_ref, out_ref, *scratch,
+):
+    chunks, ranks, blocks, slots = sizes
+    tables, halo_out, halo_in, moved_out = (
+        scratch[chunks * k : chunks * k + chunks] for k in range(4)
+    )
+    block, gathered, mixed = scratch[4 * chunks : 4 * chunks + 3]
+    hs, hr, us, ur, ms, mr, own_sem = scratch[4 * chunks + 3 :]
+    elements = dist_ref.shape[0]
+    share = elements // ranks
+    local = 6 * elements
+    low = jnp.bfloat16
+    place = lax.axis_index("space")
+    me = lax.axis_index("vel")
+    after = lax.rem(place + 1, blocks)
+    before = lax.rem(place + blocks - 1, blocks)
+    peers = [lax.rem(me + k, ranks) for k in range(1, ranks)]
+
+    barrier = pltpu.get_barrier_semaphore()
+    for other in (before, after):
+        pl.semaphore_signal(barrier, inc=1, device_id={"space": other}, device_id_type=MESH)
+    for peer in peers:
+        pl.semaphore_signal(barrier, inc=1, device_id={"vel": peer}, device_id_type=MESH)
+
+    def send(src, dst, send_sem, recv_sem, target):
+        copy = pltpu.make_async_remote_copy(
+            src_ref=src, dst_ref=dst, send_sem=send_sem, recv_sem=recv_sem,
+            device_id=target, device_id_type=MESH,
+        )
+        copy.start()
+        return copy
+
+    halos, moves, returns, owns = [], [], [], []
+    for q in range(chunks):
+        lanes = slice(256 * q, 256 * q + 256)
+        table, outgoing = tables[q], halo_out[q]
+
+        def fill(e, carry):
+            got = jnp.dot(select_ref[...], dist_ref[e, :, lanes], preferred_element_type=jnp.float32)
+            table[pl.ds(6 * e, 6)] = got.astype(low).reshape(6, 16, 256)
+            return carry
+
+        lax.fori_loop(0, elements, fill, 0)
+        for j in range(2):
+
+            def pick(m, carry):
+                live = (m < count_ref[j]).astype(low)
+                outgoing[slots * j + m] = table[send_ref[j, m]] * live
+                return carry
+
+            lax.fori_loop(0, slots, pick, 0)
+        if q == 0:
+            pl.semaphore_wait(barrier, ranks + 1)
+        for j, target in ((1, after), (0, before)):
+            halos.append(
+                send(
+                    outgoing.at[pl.ds(slots * j, slots)],
+                    halo_in[q].at[pl.ds(slots * (1 - j), slots)],
+                    hs.at[q, j], hr.at[q, j], {"space": target},
+                )
+            )
+
+    for q in range(chunks):
+        lanes = slice(256 * q, 256 * q + 256)
+        table, moved = tables[q], moved_out[q]
+        halos[2 * q].wait_recv()
+        halos[2 * q + 1].wait_recv()
+        table[local : local + 2 * slots] = halo_in[q][...]
+
+        def step(e, carry):
+            here = dist_ref[e, :, lanes]
+            block[0:64] = here
+            for face in range(6):
+                got = table[source_ref[e, face]] * mask_ref[face : face + 1, lanes]
+                block[64 + 16 * face : 80 + 16 * face] = got
+                block[160 + 16 * face : 176 + 16 * face] = got
+            parts = jnp.dot(w_ref[e], block[...], preferred_element_type=jnp.float32)
+            total = coef_ref[:, lanes] * here.astype(jnp.float32)
+            for a in range(3):
+                total = total + scale_ref[a : a + 1, lanes] * parts[64 * a : 64 * a + 64]
+            moved[e] = total.astype(low)
+            return carry
+
+        lax.fori_loop(0, elements, step, 0)
+        slot = me * chunks + q
+        for k, peer in enumerate(peers):
+            moves.append(
+                send(
+                    moved.at[pl.ds(peer * share, share)], gathered.at[slot],
+                    us.at[k, q], ur.at[k, q], {"vel": peer},
+                )
+            )
+        gathered[slot] = moved[pl.ds(me * share, share)]
+
+    for copy in moves:
+        copy.wait_recv()
+    for x in range(share):
+
+        def collide(g, carry):
+            rows = pl.ds(pl.multiple_of(16 * g, 16), 16)
+            values = gathered[:, x, rows, :].reshape(256, 256)
+            got = collide_block(
+                values, kernel_ref, pair_t_ref[...], pair_ref[...], outer_ref[...], outer_t_ref[...]
+            )
+            for s in range(ranks):
+                for q in range(chunks):
+                    at = 16 * (chunks * s + q)
+                    mixed[s, x, rows, 256 * q : 256 * q + 256] = got[at : at + 16]
+            return carry
+
+        lax.fori_loop(0, 4, collide, 0)
+        spot = me * share + x
+        for k, peer in enumerate(peers):
+            returns.append(
+                send(mixed.at[peer, x], out_ref.at[spot], ms.at[k, x], mr.at[k, x], {"vel": peer})
+            )
+        own = pltpu.make_async_copy(mixed.at[me, x], out_ref.at[spot], own_sem.at[x])
+        own.start()
+        owns.append(own)
+
+    for copy in halos + moves:
+        copy.wait_send()
+    for copy in returns:
+        copy.wait()
+    for copy in owns:
+        copy.wait()
 
 
 def on_device(dist, send_faces, send_count, source_face, subface, alpha, beta):
@@ -213,23 +274,12 @@
     vel_local = dist.shape[2]
     slots = send_faces.shape[2]
     ranks = lax.axis_size("vel")
+    blocks = lax.axis_size("space")
+    chunks = vel_local // 256
+    share = elements // ranks
     smem = pl.BlockSpec(memory_space=pltpu.SMEM)
     vmem = pl.BlockSpec(memory_space=pltpu.VMEM)
     stacked, selector = face_parts()
-    params = pltpu.CompilerParams(vmem_limit_bytes=48 * 1024 * 1024)
-
-    table, outgoing = pl.pallas_call(
-        trace_kernel,
-        out_shape=(
-            jax.ShapeDtypeStruct((elements * 6, 16, vel_local), low),
-            jax.ShapeDtypeStruct((2, slots, 16, vel_local), low),
-        ),
-        in_specs=[smem, smem, vmem, vmem],
-        out_specs=(vmem, vmem),
-        compiler_params=params,
-    )(send_faces[0], send_count[0], jnp.asarray(selector, low), dist)
-    from_prev = passed_along(outgoing[1], "space", 1)
-    from_next = passed_along(outgoing[0], "space", -1)
 
     speeds = velocity_components(lax.axis_index("vel") * vel_local, vel_local)
     column_level = jnp.concatenate(
@@ -251,18 +301,6 @@
     ).reshape(6, vel_local)
     scale = -courant * speeds
 
-    updated = pl.pallas_call(
-        transport_kernel,
-        out_shape=jax.ShapeDtypeStruct(dist.shape, low),
-        in_specs=[smem] + [vmem] * 8,
-        out_specs=vmem,
-        scratch_shapes=[
-            pltpu.VMEM((elements * 6 + 2 * slots, 16, vel_local), low),
-            pltpu.VMEM((256, vel_local), low),
-        ],
-        compiler_params=params,
-    )(source_face, dist, table, from_prev, from_next, weights, coef, scale, mask)
-
     cosine = cosine_table()
     pair = np.kron(cosine, cosine)
     outer = np.kron(cosine, np.eye(16))
@@ -270,21 +308,36 @@
     kernels = jnp.concatenate([alpha, beta], axis=0)
     kernels = kernels.reshape(kernels.shape[0], VSIDE, VSIDE * VSIDE)
 
-    share = elements // ranks
-    gathered = lax.all_to_all(
-        updated.reshape(ranks, share, 64, vel_local), "vel", split_axis=0, concat_axis=0
-    )
-    blockspec = pl.BlockSpec((ranks, 1, 16, vel_local), lambda e, g: (0, e, g, 0))
-    mixed = pl.pallas_call(
-        collide_kernel,
-        grid=(share, 4),
-        out_shape=jax.ShapeDtypeStruct(gathered.shape, low),
-        in_specs=[blockspec] + [vmem] * 5,
-        out_specs=blockspec,
-        compiler_params=params,
-    )(gathered, kernels, *tables)
-    relaxed = lax.all_to_all(mixed, "vel", split_axis=0, concat_axis=0)
-    return relaxed.reshape(dist.shape)
+    scratch = (
+        [pltpu.VMEM((6 * elements + 2 * slots, 16, 256), low)] * chunks
+        + [pltpu.VMEM((2 * slots, 16, 256), low)] * (2 * chunks)
+        + [pltpu.VMEM((elements, 64, 256), low)] * chunks
+        + [
+            pltpu.VMEM((256, 256), low),
+            pltpu.VMEM((ranks * chunks, share, 64, 256), low),
+            pltpu.VMEM((ranks, share, 64, vel_local), low),
+            pltpu.SemaphoreType.DMA((chunks, 2)),
+            pltpu.SemaphoreType.DMA((chunks, 2)),
+            pltpu.SemaphoreType.DMA((ranks - 1, chunks)),
+            pltpu.SemaphoreType.DMA((ranks - 1, chunks)),
+            pltpu.SemaphoreType.DMA((ranks - 1, share)),
+            pltpu.SemaphoreType.DMA((ranks - 1, share)),
+            pltpu.SemaphoreType.DMA((share,)),
+        ]
+    )
+    return pl.pallas_call(
+        functools.partial(fused_kernel, (chunks, ranks, blocks, slots)),
+        out_shape=jax.ShapeDtypeStruct(dist.shape, low),
+        in_specs=[smem] * 3 + [vmem] * 11,
+        out_specs=pl.BlockSpec(memory_space=pl.ANY),
+        scratch_shapes=scratch,
+        compiler_params=pltpu.CompilerParams(
+            collective_id=0, has_side_effects=True, vmem_limit_bytes=48 * 1024 * 1024
+        ),
+    )(
+        send_faces[0], send_count[0], source_face, dist, jnp.asarray(selector, low), weights, coef,
+        scale, mask, kernels, *tables,
+    )
 
 
 def solution(mesh):

time: 127 us -> 83.6 us (0.66)
  the two profiles are of different devices: /device:TPU:0 before, /device:TPU:27 now
where the time goes in v2:
time: 83.6 us; the launch traced here: 82.3 us
  Pallas kernels  75.8 us (91%)
  local copies, waits for them, and re-layouts  3.27 us (4%)
  other arithmetic  2.89 us (3%)
    pallas_call x1, Pallas kernels, on_device(): pl.pallas_call(functools.partial(fused_kernel, (chunks, ranks, blocks, sl...  75.8 us
    unnamed x28, local copies, waits for them, and re-layouts  3.08 us

profile of v2, /device:TPU:27, one launch (start us, length us, event | category | flops | bytes accessed | tf_op | source)
XLA Modules:
  0.0 82.3 jit_solution(2189600718694285305)
XLA Ops:
  0.0 0.0 copy-start.10
  0.0 0.0 copy-start.11
  0.2 0.8 %copy.25.source_ref = s32[16,6]{1,0:T(8,128)S(1)} copy(s32[16,6]{0,1:T(8,128)} %param.22) | data formatting | bytes 768 | tf_op args[3]
  1.0 0.8 copy.24
  1.8 0.1 fusion.9
  2.0 0.1 broadcast_in_dim.80
  2.1 0.1 concatenate.50
  2.2 0.1 fusion.4
  2.3 0.9 %subtract_reduce_fusion = f32[64,1024]{1,0:T(8,128)S(1)} fusion(f32[3,1024]{1,0:T(4,128)S(1)} %get-tuple-element.8, f32[3,64]{1,0:T(4,128)} %constant.107.clone, f32[3,1024]{1,0:T(4,128)S(1)} %get-tuple-element.9, f32[3,64]{1,0:T(4,128)} %constant.108.clone), kind=kLoop, calls=%fused_computation.1 | loop fusion | flops 720896 | bytes 288256 | tf_op jit(solution)/shard_map/reduce_sum | solution.py:298
  3.2 0.0 copy-start
  3.2 0.0 copy-start.1
  3.3 0.0 copy-start.2
  3.3 0.0 copy-start.3
  3.3 0.0 copy-start.4
  3.3 0.0 copy-start.5
  3.3 0.0 copy-start.6
  3.3 1.1 %pad_maximum_fusion = f32[9,4096]{1,0:T(8,128)S(1)} fusion(f32[5,4096]{1,0:T(8,128)} %param.25, f32[4,4096]{1,0:T(4,128)} %param.24), kind=kLoop, calls=%fused_computation.2 | loop fusion | flops 36864 | bytes 294912 | tf_op jit(solution)/shard_map/concatenate | solution.py:308
  4.4 0.1 copy.26
  4.6 0.5 select_select_fusion.w_ref
  5.1 0.0 copy-done
  5.1 0.0 copy-done.1
  5.1 0.0 copy-done.2
  5.1 75.8 %shard_map.181 = bf16[16,64,1024]{2,1,0:T(8,128)(2,1)S(1)} custom-call(s32[2,16]{1,0:T(2,128)S(1)} %bitcast.11, s32[2]{0:T(128)S(1)} %bitcast.12, s32[16,6]{1,0:T(8,128)S(1)} %copy.25.source_ref, bf16[16,64,1024]{2,1,0:T(8,128)(2,1)} %dist_ref.1, bf16[96,64]{1,0:T(8,128)(2,1)S(1)} %copy-done.4, bf16[16,192,256]{2,1,0:T(8,128)(2,1)S(1)} %select_select_fusion.w_ref, ...), custom_call_target="tpu_custom_call" | custom-call | tf_op jit(solution)/shard_map/pallas_call | solution.py:328
  81.0 1.3 %copy.28 = bf16[16,64,1024]{2,1,0:T(8,128)(2,1)} copy(bf16[16,64,1024]{2,1,0:T(8,128)(2,1)S(1)} %shard_map.181) | data formatting | bytes 4194304
  (24 shorter events, 0.3 us)
Async XLA Ops:
  0.0 4.5 %copy-start.7 = (bf16[192,256]{1,0:T(8,128)(2,1)S(1)}, bf16[192,256]{1,0:T(8,128)(2,1)}, u32[]{:S(2)}) copy-start(bf16[192,256]{1,0:T(8,128)(2,1)} %constant.106.clone) | copy-start | bytes 294916
  0.0 4.5 %copy-start.8 = (bf16[192,256]{1,0:T(8,128)(2,1)S(1)}, bf16[192,256]{1,0:T(8,128)(2,1)}, u32[]{:S(2)}) copy-start(bf16[192,256]{1,0:T(8,128)(2,1)} %constant.105.clone) | copy-start | bytes 294916
  0.0 4.5 %copy-start.9 = (bf16[192,256]{1,0:T(8,128)(2,1)S(1)}, bf16[192,256]{1,0:T(8,128)(2,1)}, u32[]{:S(2)}) copy-start(bf16[192,256]{1,0:T(8,128)(2,1)} %constant.104.clone) | copy-start | bytes 294916
  0.0 4.5 %copy-start.10 = (bf16[192,256]{1,0:T(8,128)(2,1)S(1)}, bf16[192,256]{1,0:T(8,128)(2,1)}, u32[]{:S(2)}) copy-start(bf16[192,256]{1,0:T(8,128)(2,1)} %constant.103.clone) | copy-start | bytes 294916
  0.0 4.5 %copy-start.11 = (bf16[192,256]{1,0:T(8,128)(2,1)S(1)}, bf16[192,256]{1,0:T(8,128)(2,1)}, u32[]{:S(2)}) copy-start(bf16[192,256]{1,0:T(8,128)(2,1)} %constant.102.clone) | copy-start | bytes 294916
  3.2 1.8 %copy-start = (bf16[256,256]{1,0:T(8,128)(2,1)S(1)}, bf16[256,256]{1,0:T(8,128)(2,1)}, u32[]{:S(2)}) copy-start(bf16[256,256]{1,0:T(8,128)(2,1)} %constant.112.clone.outer_t_ref) | copy-start | bytes 393220
  3.2 1.8 %copy-start.1 = (bf16[256,256]{1,0:T(8,128)(2,1)S(1)}, bf16[256,256]{1,0:T(8,128)(2,1)}, u32[]{:S(2)}) copy-start(bf16[256,256]{1,0:T(8,128)(2,1)} %constant.111.clone.outer_ref) | copy-start | bytes 393220
  3.3 1.8 %copy-start.2 = (bf16[256,256]{1,0:T(8,128)(2,1)S(1)}, bf16[256,256]{1,0:T(8,128)(2,1)}, u32[]{:S(2)}) copy-start(bf16[256,256]{1,0:T(8,128)(2,1)} %constant.110.clone.pair_ref) | copy-start | bytes 393220
  3.3 1.8 %copy-start.3 = (bf16[256,256]{1,0:T(8,128)(2,1)S(1)}, bf16[256,256]{1,0:T(8,128)(2,1)}, u32[]{:S(2)}) copy-start(bf16[256,256]{1,0:T(8,128)(2,1)} %constant.109.clone.pair_t_ref) | copy-start | bytes 393220
  3.3 1.8 %copy-start.4 = (bf16[96,64]{1,0:T(8,128)(2,1)S(1)}, bf16[96,64]{1,0:T(8,128)(2,1)}, u32[]{:S(2)}) copy-start(bf16[96,64]{1,0:T(8,128)(2,1)} %constant.113.clone.select_ref) | copy-start | bytes 36868
  3.3 1.8 %copy-start.5 = (s32[1,2,16]{2,1,0:T(2,128)S(1)}, s32[1,2,16]{2,1,0:T(2,128)}, u32[]{:S(2)}) copy-start(s32[1,2,16]{2,1,0:T(2,128)} %param.20) | copy-start | bytes 388
  3.3 1.8 %copy-start.6 = (s32[1,2]{1,0:T(1,128)S(1)}, s32[1,2]{1,0:T(1,128)}, u32[]{:S(2)}) copy-start(s32[1,2]{1,0:T(1,128)} %param.21) | copy-start | bytes 28

commit v3 on v2

--- a/solution.py
+++ b/solution.py
@@ -94,12 +94,6 @@
     return (gradients, selector, mortar)
 
 
-def velocity_components(first, count):
-    index_list = first + jnp.arange(count)
-    along = [index_list // (VSIDE * VSIDE), index_list // VSIDE % VSIDE, index_list % VSIDE]
-    return jnp.stack([(entry.astype(jnp.float32) + 0.5) * (2.0 / VSIDE) - 1.0 for entry in along])
-
-
 def face_parts():
     gradients, selector, mortar = static_tables()
     low = jnp.bfloat16
@@ -139,16 +133,18 @@
 
 
 def fused_kernel(
-    sizes, send_ref, count_ref, source_ref, dist_ref, select_ref, w_ref, coef_ref, scale_ref,
-    mask_ref, kernel_ref, pair_t_ref, pair_ref, outer_ref, outer_t_ref, out_ref, *scratch,
+    sizes, send_ref, count_ref, source_ref, level_ref, dist_hbm, select_ref, stack_hbm, alpha_ref,
+    beta_ref, tables_hbm, out_ref, *scratch,
 ):
     chunks, ranks, blocks, slots = sizes
     tables, halo_out, halo_in, moved_out = (
         scratch[chunks * k : chunks * k + chunks] for k in range(4)
     )
-    block, gathered, mixed = scratch[4 * chunks : 4 * chunks + 3]
-    hs, hr, us, ur, ms, mr, own_sem = scratch[4 * chunks + 3 :]
-    elements = dist_ref.shape[0]
+    rest = scratch[4 * chunks :]
+    block, gathered, mixed, dist_ref, stack_ref, turn_ref = rest[:6]
+    w_ref, coef_ref, line_ref, kernel_ref = rest[6:10]
+    hs, hr, us, ur, ls, lr, ms, mr, own_sem, in_sem = rest[10:]
+    elements, _, width = dist_ref.shape
     share = elements // ranks
     local = 6 * elements
     low = jnp.bfloat16
@@ -164,18 +160,34 @@
     for peer in peers:
         pl.semaphore_signal(barrier, inc=1, device_id={"vel": peer}, device_id_type=MESH)
 
-    def send(src, dst, send_sem, recv_sem, target):
-        copy = pltpu.make_async_remote_copy(
+    loads = [
+        pltpu.make_async_copy(
+            dist_hbm.at[:, :, pl.ds(256 * q, 256)], dist_ref.at[:, :, pl.ds(256 * q, 256)],
+            in_sem.at[q],
+        )
+        for q in range(chunks)
+    ]
+    loads.append(pltpu.make_async_copy(stack_hbm, stack_ref, in_sem.at[chunks]))
+    loads.append(pltpu.make_async_copy(tables_hbm, turn_ref, in_sem.at[chunks + 1]))
+    for copy in loads:
+        copy.start()
+
+    def remote(src, dst, send_sem, recv_sem, target):
+        return pltpu.make_async_remote_copy(
             src_ref=src, dst_ref=dst, send_sem=send_sem, recv_sem=recv_sem,
             device_id=target, device_id_type=MESH,
         )
+
+    def send(*args):
+        copy = remote(*args)
         copy.start()
         return copy
 
-    halos, moves, returns, owns = [], [], [], []
+    halos, moves, lasts = [], [], []
     for q in range(chunks):
         lanes = slice(256 * q, 256 * q + 256)
         table, outgoing = tables[q], halo_out[q]
+        loads[q].wait()
 
         def fill(e, carry):
             got = jnp.dot(select_ref[...], dist_ref[e, :, lanes], preferred_element_type=jnp.float32)
@@ -186,8 +198,8 @@
         for j in range(2):
 
             def pick(m, carry):
-                live = (m < count_ref[j]).astype(low)
-                outgoing[slots * j + m] = table[send_ref[j, m]] * live
+                live = (m < count_ref[0, j]).astype(low)
+                outgoing[slots * j + m] = table[send_ref[0, j, m]] * live
                 return carry
 
             lax.fori_loop(0, slots, pick, 0)
@@ -202,6 +214,43 @@
                 )
             )
 
+    index = lax.broadcasted_iota(jnp.int32, (1, width), 1) + me * width
+    node = lax.broadcasted_iota(jnp.int32, (64, width), 0)
+    coef = jnp.ones((64, width), jnp.float32)
+    for a in range(3):
+        along = lax.shift_right_logical(index, 8 - 4 * a) & 15
+        speed = (along.astype(jnp.float32) + 0.5) * (2.0 / VSIDE) - 1.0
+        up, down = jnp.maximum(speed, 0.0), jnp.minimum(speed, 0.0)
+        line_ref[2 * a : 2 * a + 1, :] = jnp.where(speed > 0, -1.0, 0.0)
+        line_ref[2 * a + 1 : 2 * a + 2, :] = jnp.where(speed < 0, 1.0, 0.0)
+        line_ref[8 + a : 9 + a, :] = -courant * speed
+        digit = lax.shift_right_logical(node, 4 - 2 * a) & 3
+        inflow = jnp.where(digit == 3, down, 0.0) - jnp.where(digit == 0, up, 0.0)
+        coef = coef + courant * lift_weight * inflow
+    coef_ref[...] = coef
+    modes = alpha_ref.shape[0]
+    for m in range(2 * modes + 1):
+        source, row = (alpha_ref, m) if m < modes else (beta_ref, m - modes)
+        for i in range(VSIDE):
+            kernel_ref[m, i : i + 1, :] = source[row : row + 1, 256 * i : 256 * i + 256]
+    loads[chunks].wait()
+    lane = lax.broadcasted_iota(jnp.int32, (1, 256), 1)
+    shifted = jnp.where(lane >= 160, lane - 160, lane - 64)
+    column = lax.shift_right_arithmetic(shifted, 4)
+
+    def weigh(e, carry):
+        level = jnp.zeros((1, 256), jnp.int32)
+        for face in range(6):
+            level = jnp.where(column == face, level_ref[face, e], level)
+        total = stack_ref[0] * (level == 0).astype(jnp.float32).astype(low)
+        for k in range(1, 5):
+            total = total + stack_ref[k] * (level == k).astype(jnp.float32).astype(low)
+        w_ref[e] = total
+        return carry
+
+    lax.fori_loop(0, elements, weigh, 0)
+    loads[chunks + 1].wait()
+
     for q in range(chunks):
         lanes = slice(256 * q, 256 * q + 256)
         table, moved = tables[q], moved_out[q]
@@ -213,101 +262,105 @@
             here = dist_ref[e, :, lanes]
             block[0:64] = here
             for face in range(6):
-                got = table[source_ref[e, face]] * mask_ref[face : face + 1, lanes]
+                got = table[source_ref[face, e]] * line_ref[face : face + 1, lanes].astype(low)
                 block[64 + 16 * face : 80 + 16 * face] = got
                 block[160 + 16 * face : 176 + 16 * face] = got
             parts = jnp.dot(w_ref[e], block[...], preferred_element_type=jnp.float32)
             total = coef_ref[:, lanes] * here.astype(jnp.float32)
             for a in range(3):
-                total = total + scale_ref[a : a + 1, lanes] * parts[64 * a : 64 * a + 64]
+                total = total + line_ref[8 + a : 9 + a, lanes] * parts[64 * a : 64 * a + 64]
             moved[e] = total.astype(low)
             return carry
 
         lax.fori_loop(0, elements, step, 0)
         slot = me * chunks + q
-        for k, peer in enumerate(peers):
-            moves.append(
-                send(
-                    moved.at[pl.ds(peer * share, share)], gathered.at[slot],
-                    us.at[k, q], ur.at[k, q], {"vel": peer},
+        if q < chunks - 1:
+            for k, peer in enumerate(peers):
+                moves.append(
+                    send(
+                        moved.at[pl.ds(peer * share, share)], gathered.at[slot],
+                        us.at[k, q], ur.at[k, q], {"vel": peer},
+                    )
                 )
-            )
+        else:
+            for x in range(share):
+                for k, peer in enumerate(peers):
+                    lasts.append(
+                        send(
+                            moved.at[peer * share + x], gathered.at[slot, x],
+                            ls.at[k, x], lr.at[k, x], {"vel": peer},
+                        )
+                    )
         gathered[slot] = moved[pl.ds(me * share, share)]
+
+    def returned(k, x, g):
+        rows = pl.ds(pl.multiple_of(16 * g, 16), 16)
+        return remote(
+            mixed.at[peers[k], x, rows], out_ref.at[me * share + x, rows],
+            ms.at[k, x, g], mr.at[k, x, g], {"vel": peers[k]},
+        )
+
+    def kept(x, g):
+        rows = pl.ds(pl.multiple_of(16 * g, 16), 16)
+        return pltpu.make_async_copy(
+            mixed.at[me, x, rows], out_ref.at[me * share + x, rows], own_sem.at[x, g]
+        )
 
     for copy in moves:
         copy.wait_recv()
     for x in range(share):
+        for k in range(ranks - 1):
+            lasts[(ranks - 1) * x + k].wait_recv()
 
         def collide(g, carry):
             rows = pl.ds(pl.multiple_of(16 * g, 16), 16)
             values = gathered[:, x, rows, :].reshape(256, 256)
             got = collide_block(
-                values, kernel_ref, pair_t_ref[...], pair_ref[...], outer_ref[...], outer_t_ref[...]
+                values, kernel_ref, turn_ref[0], turn_ref[1], turn_ref[2], turn_ref[3]
             )
             for s in range(ranks):
                 for q in range(chunks):
                     at = 16 * (chunks * s + q)
                     mixed[s, x, rows, 256 * q : 256 * q + 256] = got[at : at + 16]
+            for k in range(ranks - 1):
+                returned(k, x, g).start()
+            kept(x, g).start()
             return carry
 
         lax.fori_loop(0, 4, collide, 0)
-        spot = me * share + x
-        for k, peer in enumerate(peers):
-            returns.append(
-                send(mixed.at[peer, x], out_ref.at[spot], ms.at[k, x], mr.at[k, x], {"vel": peer})
-            )
-        own = pltpu.make_async_copy(mixed.at[me, x], out_ref.at[spot], own_sem.at[x])
-        own.start()
-        owns.append(own)
-
-    for copy in halos + moves:
+
+    for copy in halos + moves + lasts:
         copy.wait_send()
-    for copy in returns:
-        copy.wait()
-    for copy in owns:
-        copy.wait()
+
+    def finish(g, carry):
+        for x in range(share):
+            for k in range(ranks - 1):
+                returned(k, x, g).wait()
+            kept(x, g).wait()
+        return carry
+
+    lax.fori_loop(0, 4, finish, 0)
 
 
 def on_device(dist, send_faces, send_count, source_face, subface, alpha, beta):
     low = jnp.bfloat16
-    elements = dist.shape[0]
-    vel_local = dist.shape[2]
+    elements, _, vel_local = dist.shape
     slots = send_faces.shape[2]
     ranks = lax.axis_size("vel")
     blocks = lax.axis_size("space")
     chunks = vel_local // 256
     share = elements // ranks
+    rows = alpha.shape[0] + beta.shape[0]
     smem = pl.BlockSpec(memory_space=pltpu.SMEM)
     vmem = pl.BlockSpec(memory_space=pltpu.VMEM)
+    anywhere = pl.BlockSpec(memory_space=pl.ANY)
     stacked, selector = face_parts()
-
-    speeds = velocity_components(lax.axis_index("vel") * vel_local, vel_local)
-    column_level = jnp.concatenate(
-        [jnp.zeros((elements, 64), subface.dtype)] + [jnp.repeat(subface, 16, axis=1)] * 2, axis=1
-    )
-    weights = jnp.zeros((elements, 192, 256), low)
-    for level in range(stacked.shape[0]):
-        weights = jnp.where(
-            column_level[:, None, :] == level, jnp.asarray(stacked[level], low)[None], weights
-        )
-    digits = np.stack([np.arange(64) // 16, np.arange(64) // 4 % 4, np.arange(64) % 4])
-    first = jnp.asarray(digits == 0, jnp.float32)[:, :, None]
-    last = jnp.asarray(digits == 3, jnp.float32)[:, :, None]
-    up = jnp.maximum(speeds, 0.0)[:, None, :]
-    down = jnp.minimum(speeds, 0.0)[:, None, :]
-    coef = 1.0 + courant * lift_weight * jnp.sum(last * down - first * up, axis=0)
-    mask = jnp.stack(
-        [-(speeds > 0).astype(low), (speeds < 0).astype(low)], axis=1
-    ).reshape(6, vel_local)
-    scale = -courant * speeds
-
     cosine = cosine_table()
     pair = np.kron(cosine, cosine)
     outer = np.kron(cosine, np.eye(16))
-    tables = [jnp.asarray(t, low) for t in (pair.T, pair, outer, outer.T)]
-    kernels = jnp.concatenate([alpha, beta], axis=0)
-    kernels = kernels.reshape(kernels.shape[0], VSIDE, VSIDE * VSIDE)
-
+    turns = np.stack([pair.T, pair, outer, outer.T])
+
+    dma = pltpu.SemaphoreType.DMA
     scratch = (
         [pltpu.VMEM((6 * elements + 2 * slots, 16, 256), low)] * chunks
         + [pltpu.VMEM((2 * slots, 16, 256), low)] * (2 * chunks)
@@ -316,27 +369,32 @@
             pltpu.VMEM((256, 256), low),
             pltpu.VMEM((ranks * chunks, share, 64, 256), low),
             pltpu.VMEM((ranks, share, 64, vel_local), low),
-            pltpu.SemaphoreType.DMA((chunks, 2)),
-            pltpu.SemaphoreType.DMA((chunks, 2)),
-            pltpu.SemaphoreType.DMA((ranks - 1, chunks)),
-            pltpu.SemaphoreType.DMA((ranks - 1, chunks)),
-            pltpu.SemaphoreType.DMA((ranks - 1, share)),
-            pltpu.SemaphoreType.DMA((ranks - 1, share)),
-            pltpu.SemaphoreType.DMA((share,)),
+            pltpu.VMEM(dist.shape, low),
+            pltpu.VMEM(stacked.shape, low),
+            pltpu.VMEM(turns.shape, low),
+            pltpu.VMEM((elements, 192, 256), low),
+            pltpu.VMEM((64, vel_local), jnp.float32),
+            pltpu.VMEM((16, vel_local), jnp.float32),
+            pltpu.VMEM((rows, VSIDE, 256), jnp.float32),
         ]
+        + [dma((chunks, 2))] * 2
+        + [dma((ranks - 1, chunks))] * 2
+        + [dma((ranks - 1, share))] * 2
+        + [dma((ranks - 1, share, 4))] * 2
+        + [dma((share, 4)), dma((chunks + 2,))]
     )
     return pl.pallas_call(
         functools.partial(fused_kernel, (chunks, ranks, blocks, slots)),
         out_shape=jax.ShapeDtypeStruct(dist.shape, low),
-        in_specs=[smem] * 3 + [vmem] * 11,
-        out_specs=pl.BlockSpec(memory_space=pl.ANY),
+        in_specs=[smem] * 4 + [anywhere, vmem, anywhere, vmem, vmem, anywhere],
+        out_specs=anywhere,
         scratch_shapes=scratch,
         compiler_params=pltpu.CompilerParams(
-            collective_id=0, has_side_effects=True, vmem_limit_bytes=48 * 1024 * 1024
+            collective_id=0, has_side_effects=True, vmem_limit_bytes=56 * 1024 * 1024
         ),
     )(
-        send_faces[0], send_count[0], source_face, dist, jnp.asarray(selector, low), weights, coef,
-        scale, mask, kernels, *tables,
+        send_faces, send_count, source_face.T, subface.T, dist, jnp.asarray(selector, low),
+        jnp.asarray(stacked, low), alpha, beta, jnp.asarray(turns, low),
     )
 
 

time: 83.6 us -> 76.2 us (0.911)
  Pallas kernels: 75.8 us -> 71.7 us
  other arithmetic: 2.89 us -> 0 us
    pallas_call x1, Pallas kernels: 75.8 us -> 71.7 us  [on_device(): pl.pallas_call(functools.partial(fused_kernel, (chunks, ranks, blocks, sl...]
    concatenate x1 -> x0, other arithmetic: 1.07 us -> none  [on_device(): kernels = jnp.concatenate([alpha, beta], axis=0)]
    reduce_sum x1 -> x0, other arithmetic: 0.9 us -> none  [on_device(): jnp.sum(last * down - first * up, axis=0)]
    unnamed x28 -> x1, local copies, waits for them, and re-layouts: 3.08 us -> 3.14 us
where the time goes in v3:
time: 76.2 us; the launch traced here: 74.9 us
  Pallas kernels  71.7 us (94%)
  local copies, waits for them, and re-layouts  3.14 us (4%)
    pallas_call x1, Pallas kernels, on_device(): pl.pallas_call(functools.partial(fused_kernel, (chunks, ranks, blocks, sl...  71.7 us
    unnamed x1, local copies, waits for them, and re-layouts  3.14 us

profile of v3, /device:TPU:27, one launch (start us, length us, event | category | flops | bytes accessed | tf_op | source)
XLA Modules:
  0.0 74.9 jit_solution(16194488247605158900)
XLA Ops:
  0.0 71.7 %shard_map.100 = bf16[16,64,1024]{2,1,0:T(8,128)(2,1)} custom-call(s32[1,2,16]{2,1,0:T(2,128)} %send_ref.1, s32[1,2]{1,0:T(1,128)} %count_ref.1, s32[6,16]{1,0:T(8,128)} %bitcast.2, s32[6,16]{1,0:T(8,128)} %bitcast.3, bf16[16,64,1024]{2,1,0:T(8,128)(2,1)} %dist_hbm.1, bf16[96,64]{1,0:T(8,128)(2,1)} %constant.6.clone.select_ref, ...), custom_call_target="tpu_custom_call" | custom-call | tf_op jit(solution)/shard_map/pallas_call | solution.py:386
  71.7 3.1 %copy.12 = bf16[16,64,1024]{2,1,0:T(8,128)(2,1)} copy(bf16[16,64,1024]{2,1,0:T(8,128)(2,1)} %shard_map.100) | data formatting | bytes 4194304

commit v4 on v3

--- a/solution.py
+++ b/solution.py
@@ -136,16 +136,18 @@
     sizes, send_ref, count_ref, source_ref, level_ref, dist_hbm, select_ref, stack_hbm, alpha_ref,
     beta_ref, tables_hbm, out_ref, *scratch,
 ):
-    chunks, ranks, blocks, slots = sizes
+    spans, ranks, blocks, slots = sizes
+    chunks = len(spans)
     tables, halo_out, halo_in, moved_out = (
         scratch[chunks * k : chunks * k + chunks] for k in range(4)
     )
     rest = scratch[4 * chunks :]
-    block, gathered, mixed, dist_ref, stack_ref, turn_ref = rest[:6]
-    w_ref, coef_ref, line_ref, kernel_ref = rest[6:10]
-    hs, hr, us, ur, ls, lr, ms, mr, own_sem, in_sem = rest[10:]
+    gathered, mixed, dist_ref, stack_ref, turn_ref = rest[:5]
+    w_ref, coef_ref, line_ref, kernel_ref = rest[5:9]
+    hs, hr, us, ur, ls, lr, ms, mr, own_sem, in_sem = rest[9:]
     elements, _, width = dist_ref.shape
     share = elements // ranks
+    groups = width // 256
     local = 6 * elements
     low = jnp.bfloat16
     place = lax.axis_index("space")
@@ -162,10 +164,9 @@
 
     loads = [
         pltpu.make_async_copy(
-            dist_hbm.at[:, :, pl.ds(256 * q, 256)], dist_ref.at[:, :, pl.ds(256 * q, 256)],
-            in_sem.at[q],
+            dist_hbm.at[:, :, pl.ds(at, wide)], dist_ref.at[:, :, pl.ds(at, wide)], in_sem.at[q]
         )
-        for q in range(chunks)
+        for q, (at, wide) in enumerate(spans)
     ]
     loads.append(pltpu.make_async_copy(stack_hbm, stack_ref, in_sem.at[chunks]))
     loads.append(pltpu.make_async_copy(tables_hbm, turn_ref, in_sem.at[chunks + 1]))
@@ -184,17 +185,19 @@
         return copy
 
     halos, moves, lasts = [], [], []
-    for q in range(chunks):
-        lanes = slice(256 * q, 256 * q + 256)
+
+    def start_halo(q):
+        at, wide = spans[q]
+        lanes = slice(at, at + wide)
         table, outgoing = tables[q], halo_out[q]
         loads[q].wait()
 
         def fill(e, carry):
             got = jnp.dot(select_ref[...], dist_ref[e, :, lanes], preferred_element_type=jnp.float32)
-            table[pl.ds(6 * e, 6)] = got.astype(low).reshape(6, 16, 256)
+            table[pl.ds(6 * e, 6)] = got.astype(low).reshape(6, 16, wide)
             return carry
 
-        lax.fori_loop(0, elements, fill, 0)
+        lax.fori_loop(0, elements, fill, 0, unroll=4)
         for j in range(2):
 
             def pick(m, carry):
@@ -202,7 +205,7 @@
                 outgoing[slots * j + m] = table[send_ref[0, j, m]] * live
                 return carry
 
-            lax.fori_loop(0, slots, pick, 0)
+            lax.fori_loop(0, slots, pick, 0, unroll=4)
         if q == 0:
             pl.semaphore_wait(barrier, ranks + 1)
         for j, target in ((1, after), (0, before)):
@@ -213,6 +216,52 @@
                     hs.at[q, j], hr.at[q, j], {"space": target},
                 )
             )
+
+    def transport(q):
+        at, wide = spans[q]
+        lanes = slice(at, at + wide)
+        table, moved = tables[q], moved_out[q]
+        halos[2 * q].wait_recv()
+        halos[2 * q + 1].wait_recv()
+        table[local : local + 2 * slots] = halo_in[q][...]
+        signs = [line_ref[face : face + 1, lanes].astype(low) for face in range(6)]
+
+        def step(e, carry):
+            here = dist_ref[e, :, lanes]
+            near = [table[source_ref[face, e]] * signs[face] for face in range(6)]
+            stacked = jnp.concatenate([here] + near + near, axis=0)
+            parts = jnp.dot(w_ref[e], stacked, preferred_element_type=jnp.float32)
+            total = coef_ref[:, lanes] * here.astype(jnp.float32)
+            for a in range(3):
+                total = total + line_ref[8 + a : 9 + a, lanes] * parts[64 * a : 64 * a + 64]
+            moved[e] = total.astype(low)
+            return carry
+
+        lax.fori_loop(0, elements, step, 0, unroll=2)
+        slot = me * groups + at // 256
+        inside = pl.ds(at % 256, wide)
+        if q < chunks - 1:
+            for k, peer in enumerate(peers):
+                moves.append(
+                    send(
+                        moved.at[pl.ds(peer * share, share)], gathered.at[slot, :, :, inside],
+                        us.at[k, q], ur.at[k, q], {"vel": peer},
+                    )
+                )
+        else:
+            for x in range(share):
+                for k, peer in enumerate(peers):
+                    lasts.append(
+                        send(
+                            moved.at[peer * share + x], gathered.at[slot, x, :, inside],
+                            ls.at[k, x], lr.at[k, x], {"vel": peer},
+                        )
+                    )
+        gathered[slot, :, :, at % 256 : at % 256 + wide] = moved[pl.ds(me * share, share)]
+
+    ahead = min(3, chunks)
+    for q in range(ahead):
+        start_halo(q)
 
     index = lax.broadcasted_iota(jnp.int32, (1, width), 1) + me * width
     node = lax.broadcasted_iota(jnp.int32, (64, width), 0)
@@ -248,50 +297,13 @@
         w_ref[e] = total
         return carry
 
-    lax.fori_loop(0, elements, weigh, 0)
+    lax.fori_loop(0, elements, weigh, 0, unroll=2)
     loads[chunks + 1].wait()
 
     for q in range(chunks):
-        lanes = slice(256 * q, 256 * q + 256)
-        table, moved = tables[q], moved_out[q]
-        halos[2 * q].wait_recv()
-        halos[2 * q + 1].wait_recv()
-        table[local : local + 2 * slots] = halo_in[q][...]
-
-        def step(e, carry):
-            here = dist_ref[e, :, lanes]
-            block[0:64] = here
-            for face in range(6):
-                got = table[source_ref[face, e]] * line_ref[face : face + 1, lanes].astype(low)
-                block[64 + 16 * face : 80 + 16 * face] = got
-                block[160 + 16 * face : 176 + 16 * face] = got
-            parts = jnp.dot(w_ref[e], block[...], preferred_element_type=jnp.float32)
-            total = coef_ref[:, lanes] * here.astype(jnp.float32)
-            for a in range(3):
-                total = total + line_ref[8 + a : 9 + a, lanes] * parts[64 * a : 64 * a + 64]
-            moved[e] = total.astype(low)
-            return carry
-
-        lax.fori_loop(0, elements, step, 0)
-        slot = me * chunks + q
-        if q < chunks - 1:
-            for k, peer in enumerate(peers):
-                moves.append(
-                    send(
-                        moved.at[pl.ds(peer * share, share)], gathered.at[slot],
-                        us.at[k, q], ur.at[k, q], {"vel": peer},
-                    )
-                )
-        else:
-            for x in range(share):
-                for k, peer in enumerate(peers):
-                    lasts.append(
-                        send(
-                            moved.at[peer * share + x], gathered.at[slot, x],
-                            ls.at[k, x], lr.at[k, x], {"vel": peer},
-                        )
-                    )
-        gathered[slot] = moved[pl.ds(me * share, share)]
+        transport(q)
+        if q + ahead < chunks:
+            start_halo(q + ahead)
 
     def returned(k, x, g):
         rows = pl.ds(pl.multiple_of(16 * g, 16), 16)
@@ -319,8 +331,8 @@
                 values, kernel_ref, turn_ref[0], turn_ref[1], turn_ref[2], turn_ref[3]
             )
             for s in range(ranks):
-                for q in range(chunks):
-                    at = 16 * (chunks * s + q)
+                for q in range(groups):
+                    at = 16 * (groups * s + q)
                     mixed[s, x, rows, 256 * q : 256 * q + 256] = got[at : at + 16]
             for k in range(ranks - 1):
                 returned(k, x, g).start()
@@ -348,12 +360,14 @@
     slots = send_faces.shape[2]
     ranks = lax.axis_size("vel")
     blocks = lax.axis_size("space")
-    chunks = vel_local // 256
+    spans = [(0, 128), (128, 128)] + [(at, 256) for at in range(256, vel_local, 256)]
+    chunks = len(spans)
     share = elements // ranks
     rows = alpha.shape[0] + beta.shape[0]
     smem = pl.BlockSpec(memory_space=pltpu.SMEM)
     vmem = pl.BlockSpec(memory_space=pltpu.VMEM)
     anywhere = pl.BlockSpec(memory_space=pl.ANY)
+    hbm = pl.BlockSpec(memory_space=pltpu.HBM)
     stacked, selector = face_parts()
     cosine = cosine_table()
     pair = np.kron(cosine, cosine)
@@ -362,12 +376,11 @@
 
     dma = pltpu.SemaphoreType.DMA
     scratch = (
-        [pltpu.VMEM((6 * elements + 2 * slots, 16, 256), low)] * chunks
-        + [pltpu.VMEM((2 * slots, 16, 256), low)] * (2 * chunks)
-        + [pltpu.VMEM((elements, 64, 256), low)] * chunks
+        [pltpu.VMEM((6 * elements + 2 * slots, 16, wide), low) for _, wide in spans]
+        + [pltpu.VMEM((2 * slots, 16, wide), low) for _, wide in spans] * 2
+        + [pltpu.VMEM((elements, 64, wide), low) for _, wide in spans]
         + [
-            pltpu.VMEM((256, 256), low),
-            pltpu.VMEM((ranks * chunks, share, 64, 256), low),
+            pltpu.VMEM((ranks * vel_local // 256, share, 64, 256), low),
             pltpu.VMEM((ranks, share, 64, vel_local), low),
             pltpu.VMEM(dist.shape, low),
             pltpu.VMEM(stacked.shape, low),
@@ -384,9 +397,9 @@
         + [dma((share, 4)), dma((chunks + 2,))]
     )
     return pl.pallas_call(
-        functools.partial(fused_kernel, (chunks, ranks, blocks, slots)),
+        functools.partial(fused_kernel, (spans, ranks, blocks, slots)),
         out_shape=jax.ShapeDtypeStruct(dist.shape, low),
-        in_specs=[smem] * 4 + [anywhere, vmem, anywhere, vmem, vmem, anywhere],
+        in_specs=[smem] * 4 + [hbm, vmem, hbm, vmem, vmem, hbm],
         out_specs=anywhere,
         scratch_shapes=scratch,
         compiler_params=pltpu.CompilerParams(

time: 76.2 us -> 69.4 us (0.911); the launches traced: 74.9 us -> 69.2 us
  Pallas kernels: 71.7 us -> 66 us
    pallas_call x1, Pallas kernels: 71.7 us -> 66 us  [on_device(): pl.pallas_call(functools.partial(fused_kernel, (spans, ranks, blocks, slo...]
where the time goes in v4:
time: 69.4 us; the launch traced here: 69.2 us
  Pallas kernels  66 us (95%)
  local copies, waits for them, and re-layouts  3.14 us (5%)
    pallas_call x1, Pallas kernels, on_device(): pl.pallas_call(functools.partial(fused_kernel, (spans, ranks, blocks, slo...  66 us
    unnamed x1, local copies, waits for them, and re-layouts  3.14 us

profile of v4, /device:TPU:27, one launch (start us, length us, event | category | flops | bytes accessed | tf_op | source)
XLA Modules:
  0.0 69.2 jit_solution(14917199783145216552)
XLA Ops:
  0.0 66.0 %shard_map.100 = bf16[16,64,1024]{2,1,0:T(8,128)(2,1)} custom-call(s32[1,2,16]{2,1,0:T(2,128)} %send_ref.1, s32[1,2]{1,0:T(1,128)} %count_ref.1, s32[6,16]{1,0:T(8,128)} %bitcast.2, s32[6,16]{1,0:T(8,128)} %bitcast.3, bf16[16,64,1024]{2,1,0:T(8,128)(2,1)} %dist_hbm.1, bf16[96,64]{1,0:T(8,128)(2,1)} %constant.6.clone.select_ref, ...), custom_call_target="tpu_custom_call" | custom-call | tf_op jit(solution)/shard_map/pallas_call | solution.py:399
  66.0 3.1 %copy.12 = bf16[16,64,1024]{2,1,0:T(8,128)(2,1)} copy(bf16[16,64,1024]{2,1,0:T(8,128)(2,1)} %shard_map.100) | data formatting | bytes 4194304

commit v5 on v4

--- a/solution.py
+++ b/solution.py
@@ -324,22 +324,28 @@
         for k in range(ranks - 1):
             lasts[(ranks - 1) * x + k].wait_recv()
 
-        def collide(g, carry):
-            rows = pl.ds(pl.multiple_of(16 * g, 16), 16)
-            values = gathered[:, x, rows, :].reshape(256, 256)
-            got = collide_block(
-                values, kernel_ref, turn_ref[0], turn_ref[1], turn_ref[2], turn_ref[3]
-            )
-            for s in range(ranks):
-                for q in range(groups):
-                    at = 16 * (groups * s + q)
-                    mixed[s, x, rows, 256 * q : 256 * q + 256] = got[at : at + 16]
-            for k in range(ranks - 1):
-                returned(k, x, g).start()
-            kept(x, g).start()
+        def collide(pair_at, carry):
+            both = [2 * pair_at, 2 * pair_at + 1]
+            spots = [pl.ds(pl.multiple_of(16 * g, 16), 16) for g in both]
+            results = [
+                collide_block(
+                    gathered[:, x, rows, :].reshape(256, 256), kernel_ref, turn_ref[0],
+                    turn_ref[1], turn_ref[2], turn_ref[3],
+                )
+                for rows in spots
+            ]
+            for rows, got in zip(spots, results):
+                for s in range(ranks):
+                    for q in range(groups):
+                        at = 16 * (groups * s + q)
+                        mixed[s, x, rows, 256 * q : 256 * q + 256] = got[at : at + 16]
+            for g in both:
+                for k in range(ranks - 1):
+                    returned(k, x, g).start()
+                kept(x, g).start()
             return carry
 
-        lax.fori_loop(0, 4, collide, 0)
+        lax.fori_loop(0, 2, collide, 0)
 
     for copy in halos + moves + lasts:
         copy.wait_send()

time: 69.4 us -> 70.3 us (1.013)
  Pallas kernels: 66 us -> 67 us
    pallas_call x1, Pallas kernels: 66 us -> 67 us  [on_device(): pl.pallas_call(functools.partial(fused_kernel, (spans, ranks, blocks, slo...]
where the time goes in v5:
time: 70.3 us; the launch traced here: 70.1 us
  Pallas kernels  67 us (95%)
  local copies, waits for them, and re-layouts  3.14 us (4%)
    pallas_call x1, Pallas kernels, on_device(): pl.pallas_call(functools.partial(fused_kernel, (spans, ranks, blocks, slo...  67 us
    unnamed x1, local copies, waits for them, and re-layouts  3.14 us

profile of v5, /device:TPU:27, one launch (start us, length us, event | category | flops | bytes accessed | tf_op | source)
XLA Modules:
  0.0 70.1 jit_solution(13144307648299092510)
XLA Ops:
  0.0 67.0 %shard_map.100 = bf16[16,64,1024]{2,1,0:T(8,128)(2,1)} custom-call(s32[1,2,16]{2,1,0:T(2,128)} %send_ref.1, s32[1,2]{1,0:T(1,128)} %count_ref.1, s32[6,16]{1,0:T(8,128)} %bitcast.2, s32[6,16]{1,0:T(8,128)} %bitcast.3, bf16[16,64,1024]{2,1,0:T(8,128)(2,1)} %dist_hbm.1, bf16[96,64]{1,0:T(8,128)(2,1)} %constant.6.clone.select_ref, ...), custom_call_target="tpu_custom_call" | custom-call | tf_op jit(solution)/shard_map/pallas_call | solution.py:405
  67.0 3.1 %copy.12 = bf16[16,64,1024]{2,1,0:T(8,128)(2,1)} copy(bf16[16,64,1024]{2,1,0:T(8,128)(2,1)} %shard_map.100) | data formatting | bytes 4194304

commit v6 on v4

--- a/solution.py
+++ b/solution.py
@@ -154,7 +154,8 @@
     me = lax.axis_index("vel")
     after = lax.rem(place + 1, blocks)
     before = lax.rem(place + blocks - 1, blocks)
-    peers = [lax.rem(me + k, ranks) for k in range(1, ranks)]
+    far_first = sorted(range(1, ranks), key=lambda k: abs(2 * k - ranks))
+    peers = [lax.rem(me + k, ranks) for k in far_first]
 
     barrier = pltpu.get_barrier_semaphore()
     for other in (before, after):
@@ -361,6 +362,8 @@
     ranks = lax.axis_size("vel")
     blocks = lax.axis_size("space")
     spans = [(0, 128), (128, 128)] + [(at, 256) for at in range(256, vel_local, 256)]
+    if vel_local > 256:
+        spans[-1:] = [(vel_local - 256, 128), (vel_local - 128, 128)]
     chunks = len(spans)
     share = elements // ranks
     rows = alpha.shape[0] + beta.shape[0]

time: 69.4 us -> 69.7 us (level); the launches traced: 69.2 us -> 68.5 us
  Pallas kernels: 66 us -> 65.3 us
    pallas_call x1, Pallas kernels: 66 us -> 65.3 us  [on_device(): pl.pallas_call(functools.partial(fused_kernel, (spans, ranks, blocks, slo...]
where the time goes in v6:
time: 69.7 us; the launch traced here: 68.5 us
  Pallas kernels  65.3 us (94%)
  local copies, waits for them, and re-layouts  3.14 us (5%)
    pallas_call x1, Pallas kernels, on_device(): pl.pallas_call(functools.partial(fused_kernel, (spans, ranks, blocks, slo...  65.3 us
    unnamed x1, local copies, waits for them, and re-layouts  3.14 us

profile of v6, /device:TPU:27, one launch (start us, length us, event | category | flops | bytes accessed | tf_op | source)
XLA Modules:
  0.0 68.5 jit_solution(6523804003235212108)
XLA Ops:
  0.0 65.3 %shard_map.100 = bf16[16,64,1024]{2,1,0:T(8,128)(2,1)} custom-call(s32[1,2,16]{2,1,0:T(2,128)} %send_ref.1, s32[1,2]{1,0:T(1,128)} %count_ref.1, s32[6,16]{1,0:T(8,128)} %bitcast.2, s32[6,16]{1,0:T(8,128)} %bitcast.3, bf16[16,64,1024]{2,1,0:T(8,128)(2,1)} %dist_hbm.1, bf16[96,64]{1,0:T(8,128)(2,1)} %constant.6.clone.select_ref, ...), custom_call_target="tpu_custom_call" | custom-call | tf_op jit(solution)/shard_map/pallas_call | solution.py:402
  65.3 3.1 %copy.12 = bf16[16,64,1024]{2,1,0:T(8,128)(2,1)} copy(bf16[16,64,1024]{2,1,0:T(8,128)(2,1)} %shard_map.100) | data formatting | bytes 4194304
